TPU v7x, 256 devices: a whole 4x4x8 slice. The times are simulated.
256 devices in a mesh: gx: 16 (over y, x), gy: 16 (over z, core).
Axes of the slice: x: 4, y: 4, z: 8, core: 2. Of those that a mesh axis runs over, the one named last changes fastest.
Arguments:
- counts: int32 [2, 16, 256, 4096], P(None, None, 'gx', 'gy'), may hold values from 0 to 8
- classes: int32 [16, 256, 4096], P(None, 'gx', 'gy'), may hold values from 0 to 7
- diffusivity: float32 [2, 8], replicated, may hold values from 0.2 to 5
- cotangent: float32 [2, 16, 256, 4096], P(None, None, 'gx', 'gy'), may hold values from -1203 to 1203
Outputs:
- gradient: float32 [2, 16, 256, 4096], P(None, None, 'gx', 'gy')
All inputs are finite; a program needn't handle non-finite values.
Results may differ from a plain program's by a relative error of at most 0.00002.
Values sent between devices are 32-bit elements; how exact they have to be, the bound alone decides.
No kernel may reach another device: no remote copies, remote signals or barrier semaphores. Data moves between devices by JAX's collectives and lax.ppermute only.
A program may use at most 128 MiB of HBM per device.

v0:
```python
import jax
import jax.numpy as jnp
from jax import lax
from jax.sharding import PartitionSpec as P

LEVELS = 4
COARSE_SWEEPS = 8
CLASSES = 8


step_time = 256.0
relax = 0.8
react = 0.3


def with_halo(block, sides, width):
    for axis, dim in sides:
        count = lax.axis_size(axis)
        forward = [(i, i + 1) for i in range(count - 1)]
        backward = [(target, source) for source, target in forward]
        low = lax.ppermute(
            lax.slice_in_dim(block, block.shape[dim] - width, None, axis=dim), axis, forward
        )
        high = lax.ppermute(lax.slice_in_dim(block, 0, width, axis=dim), axis, backward)
        block = jnp.concatenate([low, block, high], axis=dim)
    return block


def harmonic(first, second):
    return 2.0 * first * second / (first + second)


def neighbours(padded):
    return (
        padded[:, 1:-1, :-2, 1:-1],
        padded[:, 1:-1, 2:, 1:-1],
        padded[:, 1:-1, 1:-1, :-2],
        padded[:, 1:-1, 1:-1, 2:],
        padded[:, :-2, 1:-1, 1:-1],
        padded[:, 2:, 1:-1, 1:-1],
    )


def level_weights(dpad, scale):
    centre = dpad[:, 1:-1, 1:-1, 1:-1]
    weights = tuple((harmonic(centre, near) * scale for near in neighbours(dpad)))
    total = weights[0]
    for item in weights[1:]:
        total = total + item
    return (weights, 1.0 + step_time * total)


def apply_operator(upad, weights, diag):
    result = diag * upad[:, 1:-1, 1:-1, 1:-1]
    for weight, near in zip(weights, neighbours(upad)):
        result = result - step_time * weight * near
    return result


def pad_depth(field):
    return jnp.pad(field, ((0, 0), (1, 1), (0, 0), (0, 0)))


def pad_depth_rows(field):
    return jnp.pad(field, ((0, 0), (1, 1), (0, 0), (1, 1)))


def field_border(field):
    return pad_depth(with_halo(field, (("gx", 2), ("gy", 3)), 1))


def coef_border(field):
    return pad_depth(with_halo(field, (("gx", 2), ("gy", 3)), 1))


def coarse_border(field):
    return pad_depth_rows(with_halo(field, (("gx", 2),), 1))


def coarsen(field):
    shape = field.shape
    return field.reshape(shape[0], shape[1] // 2, 2, shape[2] // 2, 2, shape[3] // 2, 2).mean(
        axis=(2, 4, 6)
    )


def refine(field):
    return jnp.repeat(jnp.repeat(jnp.repeat(field, 2, axis=1), 2, axis=2), 2, axis=3)


def sweep(field, rhs, weights, diag, border):
    return field + relax * (rhs - apply_operator(border(field), weights, diag)) / diag


def column_mean(resid):
    local = jnp.sum(resid, axis=(1, 2, 3), keepdims=True)
    number = resid.shape[1] * resid.shape[2] * resid.shape[3] * lax.axis_size("gx")
    return lax.psum(local, "gx") / number


def coarse_solve(rhs, dpad, scale, border, average):
    weights, diag = level_weights(dpad, scale)
    field = relax * rhs / diag
    for count in range(COARSE_SWEEPS - 1):
        field = sweep(field, rhs, weights, diag, border)
    resid = rhs - apply_operator(border(field), weights, diag)
    return field + average(resid)


def coarsest(rhs, diff):
    rows_y = rhs.shape[3]
    scale = 0.25**LEVELS
    wide_rhs, wide_diff = (
        lax.all_gather(rhs, "gy", axis=3, tiled=True),
        lax.all_gather(diff, "gy", axis=3, tiled=True),
    )
    dpad = pad_depth_rows(with_halo(wide_diff, (("gx", 2),), 1))
    field = coarse_solve(wide_rhs, dpad, scale, coarse_border, column_mean)
    return lax.dynamic_slice_in_dim(field, lax.axis_index("gy") * rows_y, rows_y, 3)


def vcycle(level, rhs, diff):
    if level == LEVELS:
        return coarsest(rhs, diff)
    weights, diag = level_weights(coef_border(diff), 0.25**level)
    field = relax * rhs / diag
    field = sweep(field, rhs, weights, diag, field_border)
    resid = rhs - apply_operator(field_border(field), weights, diag)
    field = field + refine(vcycle(level + 1, coarsen(resid), coarsen(diff)))
    field = sweep(field, rhs, weights, diag, field_border)
    return sweep(field, rhs, weights, diag, field_border)


def per_device(counts, classes, diffusivity, cotangent):
    diff = jnp.zeros(cotangent.shape, jnp.float32)
    for index in range(CLASSES):
        diff = jnp.where((classes == index)[None], diffusivity[:, index][:, None, None, None], diff)
    adjoint = vcycle(0, cotangent, diff)
    acid = 0.25 * counts[0].astype(jnp.float32)
    quench = 0.25 * counts[1].astype(jnp.float32)
    grad_acid = adjoint[0] * (1.0 - react * quench) - react * quench * adjoint[1]
    grad_quench = adjoint[1] * (1.0 - react * acid) - react * acid * adjoint[0]
    return jnp.stack([grad_acid, grad_quench])


def solution(mesh):
    in_specs = (P(None, None, "gx", "gy"), P(None, "gx", "gy"), P(), P(None, None, "gx", "gy"))
    out_specs = P(None, None, "gx", "gy")
    return jax.shard_map(
        per_device, mesh=mesh, in_specs=in_specs, out_specs=out_specs, check_vma=False
    )
```

profile of v0, /device:TPU:134, one launch (start us, length us, event | category | flops | bytes accessed | tf_op | source)
XLA Modules:
  0.0 883.8 jit_solution(51180882853258836)
XLA Ops:
  8.8 19.4 %broadcast_in_dim.248 = pred[8,2,8,2,128,2]{5,4,3,2,1,0:T(8,128)(4,1)} reshape(pred[16,16,256]{2,1,0:T(8,128)(4,1)S(1)} %get-tuple-element.80) | data formatting | bytes 131072 | tf_op jit(solution)/shard_map/jit(_where)/broadcast_in_dim | solution.py:137
  28.3 19.4 %broadcast_in_dim.245 = pred[8,2,8,2,128,2]{5,4,3,2,1,0:T(8,128)(4,1)} reshape(pred[16,16,256]{2,1,0:T(8,128)(4,1)S(1)} %get-tuple-element.81) | data formatting | bytes 131072 | tf_op jit(solution)/shard_map/jit(_where)/broadcast_in_dim | solution.py:137
  47.7 19.4 %broadcast_in_dim.242 = pred[8,2,8,2,128,2]{5,4,3,2,1,0:T(8,128)(4,1)} reshape(pred[16,16,256]{2,1,0:T(8,128)(4,1)S(1)} %get-tuple-element.75) | data formatting | bytes 131072 | tf_op jit(solution)/shard_map/jit(_where)/broadcast_in_dim | solution.py:137
  67.1 19.4 %broadcast_in_dim.239 = pred[8,2,8,2,128,2]{5,4,3,2,1,0:T(8,128)(4,1)} reshape(pred[16,16,256]{2,1,0:T(8,128)(4,1)S(1)} %get-tuple-element.76) | data formatting | bytes 131072 | tf_op jit(solution)/shard_map/jit(_where)/broadcast_in_dim | solution.py:137
  86.5 19.4 %broadcast_in_dim.236 = pred[8,2,8,2,128,2]{5,4,3,2,1,0:T(8,128)(4,1)} reshape(pred[16,16,256]{2,1,0:T(8,128)(4,1)S(1)} %get-tuple-element.77) | data formatting | bytes 131072 | tf_op jit(solution)/shard_map/jit(_where)/broadcast_in_dim | solution.py:137
  105.9 19.4 %broadcast_in_dim.233 = pred[8,2,8,2,128,2]{5,4,3,2,1,0:T(8,128)(4,1)} reshape(pred[16,16,256]{2,1,0:T(8,128)(4,1)S(1)} %get-tuple-element.78) | data formatting | bytes 131072 | tf_op jit(solution)/shard_map/jit(_where)/broadcast_in_dim | solution.py:137
  125.3 19.4 %broadcast_in_dim.230 = pred[8,2,8,2,128,2]{5,4,3,2,1,0:T(8,128)(4,1)} reshape(pred[16,16,256]{2,1,0:T(8,128)(4,1)S(1)} %get-tuple-element.79) | data formatting | bytes 131072 | tf_op jit(solution)/shard_map/jit(_where)/broadcast_in_dim | solution.py:137
  144.7 19.4 %broadcast_in_dim.227 = pred[8,2,8,2,128,2]{5,4,3,2,1,0:T(8,128)(4,1)} reshape(pred[16,16,256]{2,1,0:T(8,128)(4,1)S(1)} %get-tuple-element.74) | data formatting | bytes 131072 | tf_op jit(solution)/shard_map/jit(_where)/broadcast_in_dim | solution.py:137
  164.1 7.5 copy.568
  171.6 7.5 copy.567
  179.1 7.5 copy.566
  186.6 7.5 copy.565
  194.1 7.8 copy.564
  201.9 7.5 copy.563
  209.4 7.5 copy.562
  216.9 7.5 copy.561
  228.2 5.2 collective-permute-start.12
  233.4 5.5 div.213
  245.4 6.0 collective-permute-start.24
  258.1 5.0 collective-permute-done.2
  268.2 3.9 collective-permute-start.5
  280.7 4.4 collective-permute-start.15
  307.9 5.0 collective-permute-done.10
  316.3 35.6 %reshape.103 = f32[2,8,2,8,2,128,2]{6,5,4,3,2,1,0:T(8,128)} reshape(f32[2,16,16,256]{3,2,1,0:T(8,128)} %fusion.11) | data formatting | bytes 1048576 | tf_op jit(solution)/shard_map/reshape | solution.py:82
  351.9 12.2 %reduce_sum.95 = f32[2,8,8,128]{3,2,1,0:T(8,128)S(1)} reduce(f32[2,8,2,8,2,128,2]{6,5,4,3,2,1,0:T(8,128)} %reshape.103, f32[]{:T(128)} %constant.105.clone.1), dimensions={2,4,6}, to_apply=%region_0.1 | reduce | flops 114688 | bytes 589828 | tf_op jit(solution)/shard_map/reduce_sum | solution.py:82
  368.2 3.9 collective-permute-start.17
  380.4 4.4 collective-permute-start.27
  393.8 5.6 collective-permute-done.21
  409.5 6.3 reshape.104
  421.3 6.0 collective-permute-start.28
  430.1 6.0 collective-permute-start.36
  446.8 6.0 collective-permute-start.32
  457.3 4.4 collective-permute-start.35
  478.1 6.0 collective-permute-start.40
  501.2 6.0 collective-permute-start.44
  507.3 14.2 %all-gather.3 = f32[16,16,2]{1,2,0:T(2,128)S(1)} all-gather(f32[1,16,2]{1,2,0:T(2,128)S(1)} %multiply_bitcast_fusion), channel_id=3, replica_groups=mesh['gx'=16,'gy'=16] {'gy'}, dimensions={0}, use_global_device_ids=true | all-gather | bytes 2176 | tf_op jit(solution)/shard_map/all_gather | solution.py:115
  525.4 6.0 collective-permute-start.48
  537.4 4.2 collective-permute-done.46
  547.4 14.2 %all-gather.2 = f32[16,16,2]{1,2,0:T(2,128)S(1)} all-gather(f32[1,16,2]{1,2,0:T(2,128)S(1)} %multiply_bitcast_fusion.1), channel_id=2, replica_groups=mesh['gx'=16,'gy'=16] {'gy'}, dimensions={0}, use_global_device_ids=true | all-gather | bytes 2176 | tf_op jit(solution)/shard_map/all_gather | solution.py:114
  567.0 6.0 collective-permute-start.50
  577.3 6.3 collective-permute-start.52
  587.7 6.3 collective-permute-start.54
  598.0 6.3 collective-permute-start.56
  608.4 6.3 collective-permute-start.58
  618.8 6.3 collective-permute-start.60
  629.1 6.3 collective-permute-start.62
  640.1 6.3 collective-permute-start.64
  650.1 33.7 %psum.7 = f32[2,1,1,1]{0,3,2,1:T(1,128)} all-reduce(f32[2,1,1,1]{0,3,2,1:T(1,128)} %bitcast.200), channel_id=1, replica_groups=mesh['gx'=16,'gy'=16] {'gx'}, use_global_device_ids=true, to_apply=%region_11.12 | all-reduce | flops 2 | bytes 16 | tf_op jit(solution)/shard_map/psum | solution.py:98
  687.9 5.6 collective-permute-start.67
  708.2 5.2 collective-permute-start.71
  734.3 3.9 collective-permute-start.75
  738.2 4.0 collective-permute-start.74
  748.2 3.9 collective-permute-done.76
  755.2 6.1 collective-permute-start.78
  767.1 3.9 collective-permute-done.80
  779.8 6.3 collective-permute-start.82
  788.0 5.7 collective-permute-done.83
  798.2 4.5 collective-permute-done.84
  817.2 4.5 collective-permute-done.88
  824.5 4.0 broadcast_in_dim.264
  828.5 4.2 copy.648
  850.2 5.0 collective-permute-done.92
  860.2 3.9 collective-permute-start.95
  874.4 5.3 collective-permute-done.96
  (466 shorter events, 328.8 us)
Async XLA Ops:
  3.0 248.5 %collective-permute-start = (f32[2,16,1,256]{3,1,2,0:T(8,128)S(1)}, f32[2,16,1,256]{3,1,2,0:T(8,128)S(1)}, u32[]{:S(2)}, u32[]{:S(2)}) collective-permute-start(f32[2,16,1,256]{3,1,2,0:T(8,128)S(1)} %copy.537), channel_id=1, source_target_pairs={{0,16},{16,32},{32,48},{48,64},{64,80},{80,96},{96,112},{112,128},... | collective-permute-start | bytes 98312 | tf_op jit(solution)/shard_map/ppermute | solution.py:21
  6.4 245.4 %collective-permute-start.1 = (f32[2,16,1,256]{3,1,2,0:T(8,128)S(1)}, f32[2,16,1,256]{3,1,2,0:T(8,128)S(1)}, u32[]{:S(2)}, u32[]{:S(2)}) collective-permute-start(f32[2,16,1,256]{3,1,2,0:T(8,128)S(1)} %copy.539), channel_id=1, source_target_pairs={{16,0},{32,16},{48,32},{64,48},{80,64},{96,80},{112,96},{128,112},... | collective-permute-start | bytes 98312 | tf_op jit(solution)/shard_map/ppermute | solution.py:24
  225.5 42.6 %collective-permute-start.13 = (f32[2,8,1,128]{3,1,2,0:T(8,128)S(1)}, f32[2,8,1,128]{3,1,2,0:T(8,128)S(1)}, u32[]{:S(2)}, u32[]{:S(2)}) collective-permute-start(f32[2,8,1,128]{3,1,2,0:T(8,128)S(1)} %bitcast.190), channel_id=1, source_target_pairs={{16,0},{32,16},{48,32},{64,48},{80,64},{96,80},{112,96},{128,112},... | collective-permute-start | bytes 24584 | tf_op jit(solution)/shard_map/ppermute | solution.py:24
  228.2 17.2 %collective-permute-start.12 = (f32[2,8,1,128]{3,1,2,0:T(8,128)S(1)}, f32[2,8,1,128]{3,1,2,0:T(8,128)S(1)}, u32[]{:S(2)}, u32[]{:S(2)}) collective-permute-start(f32[2,8,1,128]{3,1,2,0:T(8,128)S(1)} %bitcast.192), channel_id=1, source_target_pairs={{0,16},{16,32},{32,48},{48,64},{64,80},{80,96},{96,112},{112,128},... | collective-permute-start | bytes 24584 | tf_op jit(solution)/shard_map/ppermute | solution.py:21
  242.2 125.4 %collective-permute-start.25 = (f32[2,4,1,64]{3,2,1,0:T(1,128)}, f32[2,4,1,64]{3,2,1,0:T(1,128)}, u32[]{:S(2)}, u32[]{:S(2)}) collective-permute-start(f32[2,4,1,64]{3,2,1,0:T(1,128)} %get-tuple-element.141), channel_id=1, source_target_pairs={{16,0},{32,16},{48,32},{64,48},{80,64},{96,80},{112,96},{128,112},... | collective-permute-start | bytes 6152 | tf_op jit(solution)/shard_map/ppermute | solution.py:24
  245.4 122.2 %collective-permute-start.24 = (f32[2,4,1,64]{3,2,1,0:T(1,128)}, f32[2,4,1,64]{3,2,1,0:T(1,128)}, u32[]{:S(2)}, u32[]{:S(2)}) collective-permute-start(f32[2,4,1,64]{3,2,1,0:T(1,128)} %get-tuple-element.140), channel_id=1, source_target_pairs={{0,16},{16,32},{32,48},{48,64},{64,80},{80,96},{96,112},{112,128},... | collective-permute-start | bytes 6152 | tf_op jit(solution)/shard_map/ppermute | solution.py:21
  253.9 9.3 %collective-permute-start.2 = (f32[2,16,18,1]{3,1,2,0:T(8,128)S(1)}, f32[2,16,18,1]{3,1,2,0:T(8,128)S(1)}, u32[]{:S(2)}, u32[]{:S(2)}) collective-permute-start(f32[2,16,18,1]{3,1,2,0:T(8,128)S(1)} %get-tuple-element.63), channel_id=1, source_target_pairs={{0,1},{1,2},{2,3},{3,4},{4,5},{5,6},{6,7},{7,8},{8,9},{9,10},{10,1... | collective-permute-start | bytes 6920 | tf_op jit(solution)/shard_map/ppermute | solution.py:21
  268.2 7.9 collective-permute-start.5
  276.2 8.9 %collective-permute-start.7 = (f32[2,16,18,1]{3,1,2,0:T(8,128)S(1)}, f32[2,16,18,1]{3,1,2,0:T(8,128)S(1)}, u32[]{:S(2)}, u32[]{:S(2)}) collective-permute-start(f32[2,16,18,1]{3,1,2,0:T(8,128)S(1)} %get-tuple-element.59), channel_id=1, source_target_pairs={{1,0},{2,1},{3,2},{4,3},{5,4},{6,5},{7,6},{8,7},{9,8},{10,9},{11,1... | collective-permute-start | bytes 6920 | tf_op jit(solution)/shard_map/ppermute | solution.py:24
  278.1 9.3 %collective-permute-start.6 = (f32[2,16,18,1]{3,1,2,0:T(8,128)S(1)}, f32[2,16,18,1]{3,1,2,0:T(8,128)S(1)}, u32[]{:S(2)}, u32[]{:S(2)}) collective-permute-start(f32[2,16,18,1]{3,1,2,0:T(8,128)S(1)} %get-tuple-element.58), channel_id=1, source_target_pairs={{0,1},{1,2},{2,3},{3,4},{4,5},{5,6},{6,7},{7,8},{8,9},{9,10},{10,1... | collective-permute-start | bytes 6920 | tf_op jit(solution)/shard_map/ppermute | solution.py:21
  280.7 11.4 %collective-permute-start.15 = (f32[2,8,10,1]{3,1,2,0:T(8,128)S(1)}, f32[2,8,10,1]{3,1,2,0:T(8,128)S(1)}, u32[]{:S(2)}, u32[]{:S(2)}) collective-permute-start(f32[2,8,10,1]{3,1,2,0:T(8,128)S(1)} %get-tuple-element.100), channel_id=1, source_target_pairs={{1,0},{2,1},{3,2},{4,3},{5,4},{6,5},{7,6},{8,7},{9,8},{10,9},{11,1... | collective-permute-start | bytes 1928 | tf_op jit(solution)/shard_map/ppermute | solution.py:24
  285.1 7.0 collective-permute-start.14
  292.2 7.9 collective-permute-start.9
  300.3 7.6 collective-permute-start.11
  303.6 9.3 %collective-permute-start.10 = (f32[2,16,18,1]{3,1,2,0:T(8,128)S(1)}, f32[2,16,18,1]{3,1,2,0:T(8,128)S(1)}, u32[]{:S(2)}, u32[]{:S(2)}) collective-permute-start(f32[2,16,18,1]{3,1,2,0:T(8,128)S(1)} %get-tuple-element.54), channel_id=1, source_target_pairs={{0,1},{1,2},{2,3},{3,4},{4,5},{5,6},{6,7},{7,8},{8,9},{9,10},{10,1... | collective-permute-start | bytes 6920 | tf_op jit(solution)/shard_map/ppermute | solution.py:21
  368.2 7.7 collective-permute-start.17
  376.0 10.7 %collective-permute-start.19 = (f32[2,8,10,1]{3,1,2,0:T(8,128)S(1)}, f32[2,8,10,1]{3,1,2,0:T(8,128)S(1)}, u32[]{:S(2)}, u32[]{:S(2)}) collective-permute-start(f32[2,8,10,1]{3,1,2,0:T(8,128)S(1)} %get-tuple-element.97), channel_id=1, source_target_pairs={{1,0},{2,1},{3,2},{4,3},{5,4},{6,5},{7,6},{8,7},{9,8},{10,9},{11,1... | collective-permute-start | bytes 1928 | tf_op jit(solution)/shard_map/ppermute | solution.py:24
  377.9 8.8 collective-permute-start.18
  380.4 8.7 collective-permute-start.27
  391.8 7.6 collective-permute-start.21
  401.5 7.0 collective-permute-start.22
  419.4 16.7 %collective-permute-start.29 = (f32[2,4,1,64]{3,2,1,0:T(1,128)S(1)}, f32[2,4,1,64]{3,2,1,0:T(1,128)S(1)}, u32[]{:S(2)}, u32[]{:S(2)}) collective-permute-start(f32[2,4,1,64]{3,2,1,0:T(1,128)S(1)} %get-tuple-element.139), channel_id=1, source_target_pairs={{16,0},{32,16},{48,32},{64,48},{80,64},{96,80},{112,96},{128,112},... | collective-permute-start | bytes 6152 | tf_op jit(solution)/shard_map/ppermute | solution.py:24
  421.3 14.8 %collective-permute-start.28 = (f32[2,4,1,64]{3,2,1,0:T(1,128)S(1)}, f32[2,4,1,64]{3,2,1,0:T(1,128)S(1)}, u32[]{:S(2)}, u32[]{:S(2)}) collective-permute-start(f32[2,4,1,64]{3,2,1,0:T(1,128)S(1)} %get-tuple-element.138), channel_id=1, source_target_pairs={{0,16},{16,32},{32,48},{48,64},{64,80},{80,96},{96,112},{112,128},... | collective-permute-start | bytes 6152 | tf_op jit(solution)/shard_map/ppermute | solution.py:21
  428.1 12.4 %collective-permute-start.37 = (f32[2,2,1,32]{3,2,1,0:T(1,128)S(1)}, f32[2,2,1,32]{3,2,1,0:T(1,128)S(1)}, u32[]{:S(2)}, u32[]{:S(2)}) collective-permute-start(f32[2,2,1,32]{3,2,1,0:T(1,128)S(1)} %get-tuple-element.162), channel_id=1, source_target_pairs={{16,0},{32,16},{48,32},{64,48},{80,64},{96,80},{112,96},{128,112},... | collective-permute-start | bytes 1544 | tf_op jit(solution)/shard_map/ppermute | solution.py:24
  430.1 10.5 %collective-permute-start.36 = (f32[2,2,1,32]{3,2,1,0:T(1,128)S(1)}, f32[2,2,1,32]{3,2,1,0:T(1,128)S(1)}, u32[]{:S(2)}, u32[]{:S(2)}) collective-permute-start(f32[2,2,1,32]{3,2,1,0:T(1,128)S(1)} %get-tuple-element.161), channel_id=1, source_target_pairs={{0,16},{16,32},{32,48},{48,64},{64,80},{80,96},{96,112},{112,128},... | collective-permute-start | bytes 1544 | tf_op jit(solution)/shard_map/ppermute | solution.py:21
  444.8 12.4 %collective-permute-start.33 = (f32[2,4,1,64]{3,2,1,0:T(1,128)S(1)}, f32[2,4,1,64]{3,2,1,0:T(1,128)S(1)}, u32[]{:S(2)}, u32[]{:S(2)}) collective-permute-start(f32[2,4,1,64]{3,2,1,0:T(1,128)S(1)} %get-tuple-element.137), channel_id=1, source_target_pairs={{16,0},{32,16},{48,32},{64,48},{80,64},{96,80},{112,96},{128,112},... | collective-permute-start | bytes 6152 | tf_op jit(solution)/shard_map/ppermute | solution.py:24
  446.8 10.5 %collective-permute-start.32 = (f32[2,4,1,64]{3,2,1,0:T(1,128)S(1)}, f32[2,4,1,64]{3,2,1,0:T(1,128)S(1)}, u32[]{:S(2)}, u32[]{:S(2)}) collective-permute-start(f32[2,4,1,64]{3,2,1,0:T(1,128)S(1)} %get-tuple-element.136), channel_id=1, source_target_pairs={{0,16},{16,32},{32,48},{48,64},{64,80},{80,96},{96,112},{112,128},... | collective-permute-start | bytes 6152 | tf_op jit(solution)/shard_map/ppermute | solution.py:21
  452.9 10.8 %collective-permute-start.39 = (f32[2,2,4,1]{3,2,1,0:T(4,128)S(1)}, f32[2,2,4,1]{3,2,1,0:T(4,128)S(1)}, u32[]{:S(2)}, u32[]{:S(2)}) collective-permute-start(f32[2,2,4,1]{3,2,1,0:T(4,128)S(1)} %get-tuple-element.151), channel_id=1, source_target_pairs={{1,0},{2,1},{3,2},{4,3},{5,4},{6,5},{7,6},{8,7},{9,8},{10,9},{11,1... | collective-permute-start | bytes 200 | tf_op jit(solution)/shard_map/ppermute | solution.py:24
  454.8 8.9 %collective-permute-start.38 = (f32[2,2,4,1]{3,2,1,0:T(4,128)S(1)}, f32[2,2,4,1]{3,2,1,0:T(4,128)S(1)}, u32[]{:S(2)}, u32[]{:S(2)}) collective-permute-start(f32[2,2,4,1]{3,2,1,0:T(4,128)S(1)} %get-tuple-element.150), channel_id=1, source_target_pairs={{0,1},{1,2},{2,3},{3,4},{4,5},{5,6},{6,7},{7,8},{8,9},{9,10},{10,1... | collective-permute-start | bytes 200 | tf_op jit(solution)/shard_map/ppermute | solution.py:21
  457.3 7.7 collective-permute-start.35
  476.2 11.3 %collective-permute-start.41 = (f32[2,2,1,32]{3,2,1,0:T(1,128)}, f32[2,2,1,32]{3,2,1,0:T(1,128)}, u32[]{:S(2)}, u32[]{:S(2)}) collective-permute-start(f32[2,2,1,32]{3,2,1,0:T(1,128)} %get-tuple-element.160), channel_id=1, source_target_pairs={{16,0},{32,16},{48,32},{64,48},{80,64},{96,80},{112,96},{128,112},... | collective-permute-start | bytes 1544 | tf_op jit(solution)/shard_map/ppermute | solution.py:24
  478.1 9.4 %collective-permute-start.40 = (f32[2,2,1,32]{3,2,1,0:T(1,128)}, f32[2,2,1,32]{3,2,1,0:T(1,128)}, u32[]{:S(2)}, u32[]{:S(2)}) collective-permute-start(f32[2,2,1,32]{3,2,1,0:T(1,128)} %get-tuple-element.159), channel_id=1, source_target_pairs={{0,16},{16,32},{32,48},{48,64},{64,80},{80,96},{96,112},{112,128},... | collective-permute-start | bytes 1544 | tf_op jit(solution)/shard_map/ppermute | solution.py:21
  499.3 32.1 %collective-permute-start.45 = (f32[2,2,1,32]{3,2,1,0:T(1,128)}, f32[2,2,1,32]{3,2,1,0:T(1,128)}, u32[]{:S(2)}, u32[]{:S(2)}) collective-permute-start(f32[2,2,1,32]{3,2,1,0:T(1,128)} %get-tuple-element.158), channel_id=1, source_target_pairs={{16,0},{32,16},{48,32},{64,48},{80,64},{96,80},{112,96},{128,112},... | collective-permute-start | bytes 1544 | tf_op jit(solution)/shard_map/ppermute | solution.py:24
  501.2 30.2 %collective-permute-start.44 = (f32[2,2,1,32]{3,2,1,0:T(1,128)}, f32[2,2,1,32]{3,2,1,0:T(1,128)}, u32[]{:S(2)}, u32[]{:S(2)}) collective-permute-start(f32[2,2,1,32]{3,2,1,0:T(1,128)} %get-tuple-element.157), channel_id=1, source_target_pairs={{0,16},{16,32},{32,48},{48,64},{64,80},{80,96},{96,112},{112,128},... | collective-permute-start | bytes 1544 | tf_op jit(solution)/shard_map/ppermute | solution.py:21
  523.4 40.1 %collective-permute-start.49 = (f32[2,1,1,256]{3,0,2,1:T(2,128)}, f32[2,1,1,256]{3,0,2,1:T(2,128)}, u32[]{:S(2)}, u32[]{:S(2)}) collective-permute-start(f32[2,1,1,256]{3,0,2,1:T(2,128)} %bitcast.150), channel_id=1, source_target_pairs={{16,0},{32,16},{48,32},{64,48},{80,64},{96,80},{112,96},{128,112},... | collective-permute-start | bytes 6152 | tf_op jit(solution)/shard_map/ppermute | solution.py:24
  525.4 38.1 %collective-permute-start.48 = (f32[2,1,1,256]{3,0,2,1:T(2,128)}, f32[2,1,1,256]{3,0,2,1:T(2,128)}, u32[]{:S(2)}, u32[]{:S(2)}) collective-permute-start(f32[2,1,1,256]{3,0,2,1:T(2,128)} %bitcast.151), channel_id=1, source_target_pairs={{0,16},{16,32},{32,48},{48,64},{64,80},{80,96},{96,112},{112,128},... | collective-permute-start | bytes 6152 | tf_op jit(solution)/shard_map/ppermute | solution.py:21
  565.1 8.0 collective-permute-start.51
  567.0 7.3 collective-permute-start.50
  575.2 8.4 collective-permute-start.53
  577.3 7.6 collective-permute-start.52
  585.8 8.2 collective-permute-start.55
  587.7 7.6 collective-permute-start.54
  596.1 8.2 collective-permute-start.57
  598.0 7.6 collective-permute-start.56
  606.5 8.2 collective-permute-start.59
  608.4 7.6 collective-permute-start.58
  616.8 8.2 collective-permute-start.61
  618.8 7.6 collective-permute-start.60
  627.2 8.2 collective-permute-start.63
  629.1 7.6 collective-permute-start.62
  638.2 8.2 collective-permute-start.65
  640.1 7.8 collective-permute-start.64
  687.9 8.0 collective-permute-start.67
  708.2 8.0 collective-permute-start.71
  734.3 8.0 collective-permute-start.75
  753.2 8.1 collective-permute-start.79
  755.2 7.5 collective-permute-start.78
  779.8 8.2 collective-permute-start.82
  786.1 7.7 collective-permute-start.83
  805.1 7.7 collective-permute-start.87
  836.0 7.9 collective-permute-start.91
  846.0 9.3 %collective-permute-start.92 = (f32[2,16,18,1]{3,1,2,0:T(8,128)S(1)}, f32[2,16,18,1]{3,1,2,0:T(8,128)S(1)}, u32[]{:S(2)}, u32[]{:S(2)}) collective-permute-start(f32[2,16,18,1]{3,1,2,0:T(8,128)S(1)} %get-tuple-element.50), channel_id=1, source_target_pairs={{0,1},{1,2},{2,3},{3,4},{4,5},{5,6},{6,7},{7,8},{8,9},{9,10},{10,1... | collective-permute-start | bytes 6920 | tf_op jit(solution)/shard_map/ppermute | solution.py:21
  860.2 7.9 collective-permute-start.95
  870.2 9.5 %collective-permute-start.96 = (f32[2,16,18,1]{3,1,2,0:T(8,128)S(1)}, f32[2,16,18,1]{3,1,2,0:T(8,128)S(1)}, u32[]{:S(2)}, u32[]{:S(2)}) collective-permute-start(f32[2,16,18,1]{3,1,2,0:T(8,128)S(1)} %get-tuple-element.46), channel_id=1, source_target_pairs={{0,1},{1,2},{2,3},{3,4},{4,5},{5,6},{6,7},{7,8},{8,9},{9,10},{10,1... | collective-permute-start | bytes 6920 | tf_op jit(solution)/shard_map/ppermute | solution.py:21
  (68 other events, 1195.8 us)
where the time goes:
time: 899 us; the launch traced here: 884 us
  local copies, waits for them, and re-layouts  311 us (35%)
  starting transfers between devices  309 us (34%)
  waiting for transfers between devices  122 us (14%)
  other arithmetic  76.8 us (9%)
  blocking collectives  62 us (7%)
    broadcast_in_dim x16, local copies, waits for them, and re-layouts, per_device(): jnp.where((classes == index)[None], diffusivity[:, index][:, None, None,...  216 us
    ppermute x49, starting transfers between devices, with_halo(): lax.ppermute(lax.slice_in_dim(block, block.shape[dim] - width, None, axis...  182 us
    ppermute x49, starting transfers between devices, with_halo(): lax.ppermute(lax.slice_in_dim(block, 0, width, axis=dim), axis, backward)  127 us
    ppermute x49, waiting for transfers between devices, with_halo(): lax.ppermute(lax.slice_in_dim(block, block.shape[dim] - width, None, axis...  83.7 us
    reshape x3, local copies, waits for them, and re-layouts, coarsen(): field.reshape(shape[0], shape[1] // 2, 2, shape[2] // 2, 2, shape[3] // 2...  44 us
    ppermute x49, waiting for transfers between devices, with_halo(): lax.ppermute(lax.slice_in_dim(block, 0, width, axis=dim), axis, backward)  38.8 us
    psum x1, blocking collectives, column_mean(): return lax.psum(local, 'gx') / number  33.7 us
    reduce_sum x9, other arithmetic, coarsen(): field.reshape(shape[0], shape[1] // 2, 2, shape[2] // 2, 2, shape[3] // 2...  23.8 us
  transfers between devices with their start and end apart: 98, of which 41 were waited for; matrix products, arithmetic and copies ran while one was open for 35% of the time, Pallas kernels for 0%

commit v1 on v0

v1 whole, which is shorter than its diff:
```python
import jax
import jax.numpy as jnp
from jax import lax
from jax.experimental import pallas as pl
from jax.experimental.pallas import tpu as pltpu
from jax.sharding import PartitionSpec as P

F32 = jnp.float32
BF16 = jnp.bfloat16
RELAX = 0.8
REACT = 0.3
STEP = 256.0
COARSE_SWEEPS = 8

HX = 4
NPL = 16 + 2 * HX
N1 = 20
HY = 64
LN = 384
PAD = 4
X2 = 64
X3 = 32
X4 = 16


def iota(shape, axis):
    return lax.broadcasted_iota(jnp.int32, shape, axis)


def shift_up(value, by, axis):
    return pltpu.roll(value, by, axis)


def shift_down(value, by, axis):
    return pltpu.roll(value, value.shape[axis] - by, axis)


def reciprocal(x):
    return pl.reciprocal(x, approx=True)


def harm(a, b):
    return a * b * reciprocal(a + b)


def residual(u, b, fx, fxn, wy, wz, sy, sz):
    fy = wy * (u - shift_up(u, sy, 1))
    mu = u + (fx - fxn) + (fy - shift_down(fy, sy, 1))
    fz = wz * (u - shift_up(u, sz, 0))
    return b - (mu + (fz - shift_down(fz, sz, 0)))


def residual_short(u, b, fx, fxn, wy, wz, sy, sz):
    fy = wy * (u - shift_up(u, sy, 1)) - shift_down(wy, sy, 1) * (shift_down(u, sy, 1) - u)
    fz = wz * (u - shift_up(u, sz, 0)) - shift_down(wz, sz, 0) * (shift_down(u, sz, 0) - u)
    return b - (u + (fx - fxn) + (fy + fz))


def diagonal(wx, wxn, wy, wz, sy, sz):
    return 1.0 + (wx + wxn) + (wy + shift_down(wy, sy, 1)) + (wz + shift_down(wz, sz, 0))


def pair_lanes(value, half):
    width = value.shape[1]
    total = value + shift_down(value, half, 1)
    first = (iota(value.shape, 1) // half) % 2 == 0
    return jnp.where(first, total, shift_up(total, half, 1))


def pair_rows(value, half):
    total = value + shift_down(value, half, 0)
    first = (iota(value.shape, 0) // half) % 2 == 0
    return jnp.where(first, total, shift_up(total, half, 0))


def split_store(ref, value):
    for k in range(value.shape[1] // 128):
        ref[k] = value[:, 128 * k : 128 * (k + 1)]


def sum_depth(ref, value):
    rows = value.shape[0]
    split_store(ref, value)
    parts = [
        ref[k, pl.ds(0, rows // 2, stride=2), :] + ref[k, pl.ds(1, rows // 2, stride=2), :]
        for k in range(value.shape[1] // 128)
    ]
    return jnp.concatenate(parts, axis=1)


def spread_depth(ref, value):
    rows = value.shape[0]
    for k in range(3):
        part = value[:, 128 * k : 128 * (k + 1)]
        ref[k, pl.ds(0, rows, stride=2), :] = part
        ref[k, pl.ds(1, rows, stride=2), :] = part
    return jnp.concatenate([ref[k] for k in range(3)], axis=1)


def pick_lanes(value, lanes):
    return jnp.take_along_axis(value, jnp.broadcast_to(lanes, value.shape), axis=1)


def stencil(u, b, wx, wy, wz, start, count, sy, sz):
    here = u[start]
    fx = wx[start] * (here - u[start - 1])
    for j in range(count):
        p = start + j
        after = u[p + 1]
        fxn = wx[p + 1] * (after - here)
        yield p, here, residual(here, b[p], fx, fxn, wy[p], wz[p], sy, sz)
        here, fx = after, fxn


def face_weights(d, wx, wy, wz, inv, b, u, start, count, factor_x, my, mz, sy, sz):
    here = d[start]
    side = factor_x(start) * harm(here, d[start - 1])
    for j in range(count):
        p = start + j
        after = d[p + 1]
        siden = factor_x(p + 1) * harm(after, here)
        y = my * harm(here, shift_up(here, sy, 1))
        z = mz * harm(here, shift_up(here, sz, 0))
        wx[p], wy[p], wz[p] = side, y, z
        value = RELAX * reciprocal(diagonal(side, siden, y, z, sy, sz))
        inv[p] = value
        u[p] = value * b[p]
        here, side = after, siden


def blocks(lo, hi, size, body):
    assert (hi - lo) % size == 0
    if hi - lo == size:
        body(lo)
        return

    def step(n, carry):
        body(lo + n * size)
        return carry

    lax.fori_loop(0, (hi - lo) // size, step, 0)


def table_kernel(diff_ref, table):
    for s in range(2):
        for c in range(8):
            table[pl.ds(8 * s + c, 1), :] = jnp.full((1, 128), diff_ref[s, c], F32)


def turn_kernel(cot, cls, table_in, own, across, inside, table):
    table[...] = table_in[...]
    odd = lax.axis_index("gy") % 2 == 1
    left_half = iota((16, 128), 1) < HY
    for f in range(3):
        for k in range(8):
            pair = []
            for x in (k, k + 8):
                pair.append(cls[:, x, :].astype(F32) if f == 2 else cot[f, :, x, :])
                own[x, f] = pair[-1]
            a, b = pair
            to_left = jnp.where(left_half, a[:, :128], pltpu.roll(b[:, :128], HY, 1))
            to_right = jnp.where(left_half, pltpu.roll(b[:, 128:], HY, 1), a[:, 128:])
            across[k, f] = jnp.where(odd, to_right, to_left)
            inside[k, f] = jnp.where(odd, to_left, to_right)


def cut_strips(planes, first, second):
    odd = lax.axis_index("gx") % 2 == 1
    for f in range(3):
        place = 0 if f == 2 else HX + f * (HX - 1)
        count = HX if f == 2 else HX - 1
        for n in range(count):
            low, high = planes[n, f], planes[16 - count + n, f]
            first[place + n] = jnp.where(odd, high, low)
            second[place + n] = jnp.where(odd, low, high)


def edge_kernel(across, inside, edge, first, second):
    odd = lax.axis_index("gy") % 2 == 1
    left_half = iota((16, 128), 1) < HY
    for k in range(8):
        for f in range(3):
            got = across[k, f], inside[k, f]
            fl, fr = jnp.where(odd, got[1], got[0]), jnp.where(odd, got[0], got[1])
            edge[k, f] = jnp.where(left_half, fr, fl)
            edge[k + 8, f] = pltpu.roll(jnp.where(left_half, fl, fr), HY, 1)
    cut_strips(edge, first, second)


def fine_tools(table, keep0, keep1, d0, v0, d1, zs):
    gx = lax.axis_index("gx")
    gy = lax.axis_index("gy")
    nx = 16 * lax.axis_size("gx")
    ny = 256 * lax.axis_size("gy")
    b0, u0, b1 = keep0.at[0], keep0.at[5], keep1.at[0]

    def look_up(values):
        cls = values.astype(jnp.int32)
        bits = [(cls & (1 << n)) != 0 for n in range(3)]
        out = []
        for s in range(2):
            rows = [jnp.broadcast_to(table[pl.ds(8 * s + c, 1), :], (16, 128)) for c in range(8)]
            rows = [jnp.concatenate([r] * (cls.shape[1] // 128), axis=1) for r in rows]
            rows = [jnp.where(bits[0], rows[2 * n + 1], rows[2 * n]) for n in range(4)]
            rows = [jnp.where(bits[1], rows[2 * n + 1], rows[2 * n]) for n in range(2)]
            out.append(jnp.where(bits[2], rows[1], rows[0]))
        return out

    def assemble_own(own, edge, size):
        def body(start):
            for j in range(size):
                x = start + j
                planes = [jnp.concatenate([own[x, f], edge[x, f]], axis=1) for f in range(3)]
                for s, d in enumerate(look_up(planes[2])):
                    b0[s, x + HX] = planes[s]
                    d0[s, x + HX] = d

        blocks(0, 16, size, body)

    def assemble_strip(main, side, high):
        second = (gx + high) % 2 == 1

        def plane(n):
            return jnp.concatenate(
                [jnp.where(second, b[n], a[n]) for a, b in (main, side)], axis=1
            )

        lo = 20 * high
        for j in range(HX):
            for s, d in enumerate(look_up(plane(j))):
                d0[s, lo + j] = d
        for s in range(2):
            for n in range(HX - 1):
                b0[s, lo + 1 - high + n] = plane(HX + s * (HX - 1) + n)

    def masks(rows, step, factor, origin):
        lane = iota((rows, LN), 1)
        ypos = gy * 256 + jnp.where(lane < 256 + HY, lane, lane - LN)
        my = jnp.where((ypos >= step) & (ypos < ny), F32(factor), F32(0.0))
        mz = jnp.where(iota((rows, LN), 0) >= 1, F32(factor), F32(0.0))

        def factor_x(p):
            xpos = (gx * 16) // step + p - origin
            return jnp.where((xpos >= 1) & (xpos < nx // step), F32(factor), F32(0.0))

        return my, mz, factor_x

    def weigh(lo, hi, size, rows, step, factor, d, keep, v):
        blocks(lo, hi, size, weigher(size, rows, step, factor, d, keep, v))

    def weigher(size, rows, step, factor, d, keep, v):
        my, mz, factor_x = masks(rows, step, factor, HX if step == 1 else 6)

        def body(start):
            for s in range(2):
                face_weights(
                    d.at[s], keep.at[1, s], keep.at[2, s], keep.at[3, s], keep.at[4, s],
                    keep.at[0, s], v.at[s], start, size, factor_x, my, mz, step, 1,
                )

        return body

    def planes(keep, u, s, start, size, step):
        return stencil(
            u.at[s], keep.at[0, s], keep.at[1, s], keep.at[2, s], keep.at[3, s],
            start, size, step, 1,
        )

    def smooth(lo, hi, size, keep, v, step):
        blocks(lo, hi, size, smoother(size, keep, v, step))

    def smoother(size, keep, v, step):
        def body(start):
            for s in range(2):
                for p, here, r in planes(keep, v, s, start, size, step):
                    keep[5, s, p] = here + keep[4, s, p] * r

        return body

    def restrict(lo, hi, size):
        blocks(lo, hi, size, restricter(size))

    def restricter(size):
        def body(start):
            for s in range(2):
                res = [r for _, _, r in planes(keep0, u0, s, 2 * start - 8, 2 * size, 1)]
                for i in range(size):
                    total = pair_lanes(res[2 * i] + res[2 * i + 1], 1)
                    b1[s, start + i] = 0.125 * sum_depth(zs.at[s, i], total)

        return body

    def coarse_diff(lo, hi, size):
        def body(start):
            for i in range(size):
                for s in range(2):
                    p = 2 * (start + i) - 8
                    total = pair_lanes(d0[s, p] + d0[s, p + 1], 1)
                    d1[s, start + i] = 0.125 * sum_depth(zs.at[s, i], total)

        blocks(lo, hi, size, body)

    at = assemble_strip, weigher, smoother, restricter
    return assemble_own, at, weigh, smooth, restrict, coarse_diff, planes


FINE = 2.0 * STEP
COARSER = 0.5 * STEP


def own_kernel(table, own, edge, keep0, keep1, d0, v0, d1, zs):
    assemble_own, _, weigh, smooth, restrict, coarse_diff, _ = fine_tools(
        table, keep0, keep1, d0, v0, d1, zs
    )
    assemble_own(own, edge, 4)
    weigh(5, 19, 7, 16, 1, FINE, d0, keep0, v0)
    smooth(6, 18, 4, keep0, v0, 1)
    restrict(8, 12, 2)
    coarse_diff(6, 14, 4)


def near_kernel(
    table, mfirst, msecond, sfirst, ssecond, keep0_in, keep1_in, d0_in, v0_in, d1_in,
    first, second, keep0, keep1, d0, v0, d1,
    zs,
):
    _, at, _, _, _, _, _ = fine_tools(table, keep0, keep1, d0, v0, d1, zs)
    assemble_strip, weigher, smoother, restricter = at
    weigh = weigher(4, 16, 1, FINE, d0, keep0, v0)
    smooth = smoother(4, keep0, v0, 1)
    restrict = restricter(2)

    def one_side(high, carry):
        assemble_strip((mfirst, msecond), (sfirst, ssecond), high)
        weigh(1 + 18 * high)
        smooth(2 + 16 * high)
        restrict(6 + 6 * high)
        return carry

    lax.fori_loop(0, 2, one_side, 0)
    odd = lax.axis_index("gx") % 2 == 1
    even_lane = iota((8, LN), 1) % 2 == 0

    def send(n, ref, low, high):
        low, high = (jnp.where(even_lane, ref[0, m], ref[1, m]) for m in (low, high))
        first[n] = jnp.where(odd, high, low)
        second[n] = jnp.where(odd, low, high)

    for k in range(4):
        send(k, keep1.at[0], 6 + k, 10 + k)
    for k in range(5):
        send(4 + k, d1, 6 + k, 9 + k)


def averaging(shape, dtype):
    group = iota(shape, 0) // 4
    target = jnp.where(group < (256 + HY) // 4, group + 16, group - 80)
    return jnp.where(iota(shape, 1) == target, F32(0.0625), F32(0.0)).astype(dtype)


def to_level2(rows, matrix, zs, message):
    rows = jnp.concatenate(rows, axis=0)
    high = rows.astype(BF16)
    rest = rows - high.astype(F32)
    middle = rest.astype(BF16)
    low = (rest - middle.astype(F32)).astype(BF16)
    whole = jnp.dot(
        jnp.concatenate([high, middle, low], axis=0), matrix, preferred_element_type=F32
    )
    whole = whole[0:64] + whole[64:128] + whole[128:192]
    lane = iota((8, 128), 1)
    halved = []
    for n in range(4):
        part = zs.at[0, n, 0]
        part[...] = whole[16 * n : 16 * (n + 1)]
        halved.append(part[pl.ds(0, 8, stride=2), :] + part[pl.ds(1, 8, stride=2), :])
    for k in range(3):
        message[k] = jnp.where(lane < 96, halved[k], pltpu.roll(halved[3], 96 - 32 * k, 1))


def inner_kernel(keep1_in, d1, counts, keep1, v1, react, diff2, matrix, zs):
    _, _, weigh, smooth, _, _, _ = fine_tools(None, keep1, keep1, None, None, d1, zs)
    weigh(7, 13, 6, 8, 2, COARSER, d1, keep1, v1)
    smooth(8, 12, 4, keep1, v1, 2)
    for s in range(2):
        for x in range(16):
            react[x, s] = REACT * (0.25 * counts[s, :, x, :].astype(F32))
    matrix[...] = averaging((LN, 128), BF16)
    rows = [d1[s, 6 + 2 * n] + d1[s, 7 + 2 * n] for n in range(4) for s in range(2)]
    to_level2(rows, matrix[...], zs, diff2)


def outer_kernel(
    first, second, diff2, matrix, keep1_in, v1_in, d1_in,
    message, keep1, v1, d1,
    zs,
):
    _, _, weigh, smooth, _, _, planes = fine_tools(None, keep1, keep1, None, None, d1, zs)
    gx = lax.axis_index("gx")
    last = lax.axis_size("gx") - 1
    odd = gx % 2 == 1
    even_lane = iota((8, LN), 1) % 2 == 0

    def both(got, ref, m, real=None):
        if real is not None:
            got = jnp.where(real, got, F32(1.0))
        ref[0, m] = jnp.where(even_lane, got, shift_up(got, 1, 1))
        ref[1, m] = jnp.where(even_lane, shift_down(got, 1, 1), got)

    for k in range(9):
        low = jnp.where(odd, second[k], first[k])
        high = jnp.where(odd, first[k], second[k])
        if k < 4:
            both(low, keep1.at[0], 2 + k)
            both(high, keep1.at[0], 14 + k)
        else:
            both(low, d1, k - 3, gx > 0)
            both(high, d1, 10 + k, gx < last)
    for start in (2, 13):
        weigh(start, start + 5, 5, 8, 2, COARSER, d1, keep1, v1)
    for start in (3, 12):
        smooth(start, start + 5, 5, keep1, v1, 2)
    res = [[r for _, _, r in planes(keep1, keep1.at[5], s, 6, 8, 2)] for s in range(2)]
    rows = [res[s][2 * n] + res[s][2 * n + 1] for n in range(4) for s in range(2)]
    to_level2(rows, matrix[...], zs, message.at[0])
    message[1] = diff2[...]


def middle_kernel(gathered, tile, keep2, keep3, d2, d3, v2, v3, coarse):
    gy = lax.axis_index("gy")
    ny = 256 * lax.axis_size("gy")
    lane = iota((8, 128), 1)
    row = iota((8, 128), 0)
    ypos = gy * 64 + lane - 16
    zero = jnp.zeros((8, 128), F32)

    for keep, d, v, count in ((keep2, d2, v2, X2), (keep3, d3, v3, X3)):
        for k in range(PAD):
            for n in range(6):
                keep[n, k] = zero
                keep[n, count + PAD + k] = zero
        for p in (PAD - 1, PAD + count):
            d[p] = zero + 1.0
            v[p] = zero

    def level(keep, d, v, count, size, sy, sz, scale, nyl):
        factor = 2.0 * STEP * scale
        my = jnp.where((ypos >= sy) & (ypos < nyl), F32(factor), F32(0.0))
        mz = jnp.where(row % 4 >= sz, F32(factor), F32(0.0))

        def factor_x(p):
            return jnp.where((p > PAD) & (p < PAD + count), F32(factor), F32(0.0))

        def weights(start):
            face_weights(
                d, keep.at[1], keep.at[2], keep.at[3], keep.at[4], keep.at[0], v,
                start, size, factor_x, my, mz, sy, sz,
            )

        def planes(u, start, amount):
            return stencil(
                u, keep.at[0], keep.at[1], keep.at[2], keep.at[3], start, amount, sy, sz
            )

        def smooth(start):
            for p, here, r in planes(v, start, count):
                keep[5, p] = here + keep[4, p] * r

        blocks(PAD, PAD + count, size, weights)
        blocks(PAD, PAD + count, count, smooth)
        return planes

    for g in range(X2 // 4):
        for f, ref in ((0, keep2.at[0]), (1, d2)):
            packed = [gathered[g, f, k] for k in range(3)]
            fourth = [pltpu.roll(packed[k], 32 * (k + 1), 1) for k in range(3)]
            fourth = jnp.where(lane < 32, fourth[0], jnp.where(lane < 64, fourth[1], fourth[2]))
            for k, plane in enumerate(packed + [fourth]):
                ref[PAD + 4 * g + k] = plane
    planes2 = level(keep2, d2, v2, X2, 32, 1, 1, 0.0625, ny // 4)

    def restrict(start):
        first = 2 * (start - PAD) + PAD
        res = [r for _, _, r in planes2(keep2.at[5], first, 32)]
        for i in range(16):
            total = res[2 * i] + res[2 * i + 1]
            keep3[0, start + i] = 0.125 * pair_rows(pair_lanes(total, 1), 1)
            total = d2[first + 2 * i] + d2[first + 2 * i + 1]
            d3[start + i] = 0.125 * pair_rows(pair_lanes(total, 1), 1)

    blocks(PAD, PAD + X3, 16, restrict)
    planes3 = level(keep3, d3, v3, X3, 32, 2, 2, 0.015625, ny // 4)

    def gather_pair(total):
        total = total + shift_down(total, 2, 1)
        return total + shift_down(total, 2, 0)

    res = [r for _, _, r in planes3(keep3.at[5], PAD, X3)]
    for i in range(X4):
        coarse[0, pl.ds(8 * i, 8), :] = gather_pair(res[2 * i] + res[2 * i + 1])
        coarse[1, pl.ds(8 * i, 8), :] = gather_pair(d3[PAD + 2 * i] + d3[PAD + 2 * i + 1])
    total = jnp.zeros((8, 128), F32)
    for g in range(8):
        f, s, half = g // 4, (g // 2) % 2, g % 2
        part = coarse[f, pl.ds(64 * half + 4 * s, 8, stride=8), :]
        part = pick_lanes(part, 16 + 4 * (lane % 16))
        total = jnp.where(lane // 16 == g, part, total)
    tile[...] = 0.125 * total


def coarsest(tiles):
    ngy = tiles.shape[0]
    width = 16 * ngy
    lane_group = iota((8, 128), 1) // 16
    fields = []
    for g in range(8):
        halves = []
        for h in range(width // 128):
            total = jnp.zeros((8, 128), F32)
            for q in range(8):
                piece = tiles[8 * h + q]
                shift = (16 * q - 16 * g) % 128
                if shift:
                    piece = pltpu.roll(piece, shift, 1)
                total = jnp.where(lane_group == q, piece, total)
            halves.append(total)
        fields.append(jnp.concatenate(halves, axis=1))
    whole = [jnp.concatenate([fields[2 * n], fields[2 * n + 1]], axis=0) for n in range(4)]
    shape = whole[0].shape
    factor = 2.0 * STEP * 0.25**4
    mx = jnp.where(iota(shape, 0) >= 1, F32(factor), F32(0.0))
    my = jnp.where(iota(shape, 1) >= 1, F32(factor), F32(0.0))
    out = []
    for s in range(2):
        b, d = whole[s], whole[2 + s]
        wx = mx * harm(d, shift_up(d, 1, 0))
        wy = my * harm(d, shift_up(d, 1, 1))
        inv = RELAX / (1.0 + (wx + shift_down(wx, 1, 0)) + (wy + shift_down(wy, 1, 1)))

        u = start = inv * b
        up_x, down_x = inv * wx, inv * shift_down(wx, 1, 0)
        up_y, down_y = inv * wy, inv * shift_down(wy, 1, 1)
        for _ in range(COARSE_SWEEPS - 1):
            along_x = up_x * shift_up(u, 1, 0) + down_x * shift_down(u, 1, 0)
            along_y = up_y * shift_up(u, 1, 1) + down_y * shift_down(u, 1, 1)
            u = ((1.0 - RELAX) * u + start) + (along_x + along_y)
        out.append(u + jnp.sum(b - u) / (shape[0] * shape[1]))
    return out


def up_kernel(
    tiles, keep2, keep3, keep0, keep1, react,
    out,
    c4, rep2, u3, u2, c2, p1, q1, q0, zs,
):
    gx = lax.axis_index("gx")
    gy = lax.axis_index("gy")

    solved = jnp.concatenate(coarsest(tiles), axis=0)
    width = solved.shape[1]
    solved = pltpu.roll(solved, (width + 4 - 16 * gy) % width, 1)[:, :128]
    near = pick_lanes(solved, iota((1, 128), 1) // 4)
    for t in range(2):
        c4[t, pl.ds(0, 8), :] = jnp.zeros((8, 128), F32)
        c4[t, pl.ds(8, X4), :] = near[X4 * t : X4 * (t + 1)]
        c4[t, pl.ds(8 + X4, 8), :] = jnp.zeros((8, 128), F32)
    first_species = iota((8, 128), 0) < 4

    def coarse_plane(k):
        rows = [
            jnp.broadcast_to(c4[t, pl.ds(gx + 6 + k, 1), :], (8, 128)) for t in range(2)
        ]
        return jnp.where(first_species, rows[0], rows[1])

    def sweeps(keep, base, u, count, sy, sz):
        for turn in range(2):
            lo, hi = 1 + turn, count - 1 - turn
            here = u[lo]
            fx = keep[1, base + lo] * (here - u[lo - 1])
            for i in range(lo, hi):
                after = u[i + 1]
                fxn = keep[1, base + i + 1] * (after - here)
                r = residual_short(
                    here, keep[0, base + i], fx, fxn,
                    keep[2, base + i], keep[3, base + i], sy, sz,
                )
                u[i] = here + keep[4, base + i] * r
                here, fx = after, fxn

    base3 = gx * 2
    for i in range(0, 10, 2):
        plane = coarse_plane(i // 2)
        u3[i] = keep3[5, base3 + i] + plane
        u3[i + 1] = keep3[5, base3 + i + 1] + plane
    sweeps(keep3, base3, u3, 10, 2, 2)
    base2 = gx * 4
    for i in range(12):
        u2[i] = keep2[5, base2 + i] + u3[min(2 + i // 2, 9)]
    sweeps(keep2, base2, u2, 12, 1, 1)

    for i in range(8):
        for k in range(2):
            rep2[pl.ds(16 * i + k, 8, stride=2), :] = u2[2 + i]
    quarter = iota((1, 128), 1) // 4
    edge = jnp.where(quarter < 16, quarter + 80, quarter - 16)
    flat = [pick_lanes(rep2[...], lanes) for lanes in (quarter + 16, quarter + 48, edge)]
    flat = jnp.concatenate(flat, axis=1)
    c2[...] = flat.reshape(8, 2, 8, LN)

    def planes(keep, u, s, start, size, step):
        return stencil(
            u.at[s], keep.at[0, s], keep.at[1, s], keep.at[2, s], keep.at[3, s],
            start, size, step, 1,
        )

    def smooth(lo, hi, size, keep, u, new, step):
        def body(start):
            for s in range(2):
                for p, here, r in planes(keep, u, s, start, size, step):
                    new[s, p] = here + keep[4, s, p] * r

        blocks(lo, hi, size, body)

    for i in range(3, 17):
        for s in range(2):
            p1[s, i] = keep1[5, s, i] + c2[(i - 6) // 2 + 2, s]
    smooth(4, 16, 12, keep1, p1, q1, 2)
    smooth(5, 15, 10, keep1, q1, p1, 2)

    def corrected_sweep(n, carry):
        start = 3 + 6 * n
        for s in range(2):
            spread = [spread_depth(zs.at[s, j], p1[s, 5 + 3 * n + j]) for j in range(4)]
            u = [keep0[5, s, start - 1 + j] + spread[j // 2] for j in range(8)]
            fx = keep0[1, s, start] * (u[1] - u[0])
            for j in range(6):
                p = start + j
                fxn = keep0[1, s, p + 1] * (u[j + 2] - u[j + 1])
                r = residual(
                    u[j + 1], keep0[0, s, p], fx, fxn, keep0[2, s, p], keep0[3, s, p], 1, 1
                )
                q0[s, p] = u[j + 1] + keep0[4, s, p] * r
                fx = fxn
        return carry

    lax.fori_loop(0, 3, corrected_sweep, 0)

    def last(start):
        adj = [[], []]
        for s in range(2):
            for p, here, r in planes(keep0, q0, s, start, 4, 1):
                adj[s].append((here + keep0[4, s, p] * r)[:, :256])
        for j in range(4):
            x = start + j - HX
            a0, a1 = adj[0][j], adj[1][j]
            total = a0 + a1
            out[0, :, x, :] = a0 - react[x, 1] * total
            out[1, :, x, :] = a1 - react[x, 0] * total

    blocks(4, 20, 4, last)


def call(
    kernel, outs, scratch, args, name, limit, kinds=None, aliases=None, cycles=0, dtypes=None
):
    spaces = {"v": pltpu.VMEM, "s": pltpu.SMEM}
    specs = [pl.BlockSpec(memory_space=spaces[k]) for k in kinds or "v" * len(args)]
    return pl.pallas_call(
        kernel,
        out_shape=[jax.ShapeDtypeStruct(o, d) for o, d in zip(outs, dtypes or [F32] * len(outs))],
        in_specs=specs,
        out_specs=[pl.BlockSpec(memory_space=pltpu.VMEM)] * len(outs),
        scratch_shapes=[pltpu.VMEM(s, F32) if isinstance(s, tuple) else s for s in scratch],
        input_output_aliases=aliases or {},
        compiler_params=pltpu.CompilerParams(vmem_limit_bytes=limit * 1024 * 1024),
        cost_estimate=pl.CostEstimate(flops=cycles, bytes_accessed=0, transcendentals=0)
        if cycles
        else None,
        name=name,
    )(*args)


def swap(axis, first, block):
    pairs = [(i, i + 1) for i in range(first, lax.axis_size(axis) - 1, 2)]
    return lax.ppermute(block, axis, pairs + [(j, i) for i, j in pairs])


def everyone(block, axis):
    count = lax.axis_size(axis)
    copies = jnp.broadcast_to(block[None], (count,) + block.shape)
    return lax.all_to_all(copies, axis, split_axis=0, concat_axis=0, tiled=True)


def per_device(counts, classes, diffusivity, cotangent):
    (table,) = call(table_kernel, [(16, 128)], [], (diffusivity,), "table", 8, "s", cycles=10**9)
    own, across, inside, table = call(
        turn_kernel,
        [(16, 3, 16, 256), (8, 3, 16, 128), (8, 3, 16, 128), (16, 128)], [],
        (cotangent, classes, table), "turn", 8,
    )
    across, inside = swap("gy", 1, across), swap("gy", 0, inside)
    strip = (3 * HX - 2, 16, 256)
    mfirst, msecond = call(cut_strips, [strip, strip], [], (own,), "strips", 8)
    mfirst, msecond = swap("gx", 1, mfirst), swap("gx", 0, msecond)
    strip = (3 * HX - 2, 16, 128)
    edge, sfirst, ssecond = call(
        edge_kernel, [(16, 3, 16, 128), strip, strip], [], (across, inside), "edge", 8
    )
    sfirst, ssecond = swap("gx", 1, sfirst), swap("gx", 0, ssecond)
    fine = [(6, 2, NPL, 16, LN), (6, 2, N1, 8, LN)]
    fine += [(2, NPL, 16, LN)] * 2 + [(2, N1, 8, LN)]
    zs = (2, 4, 3, 16, 128)
    kept = call(own_kernel, fine, [zs], (table, own, edge), "own", 8, cycles=10**7)
    strip = (9, 8, LN)
    first, second, keep0, keep1, _, _, d1 = call(
        near_kernel,
        [strip, strip] + fine, [zs],
        (table, mfirst, msecond, sfirst, ssecond, *kept), "near", 8,
        aliases={5 + n: 2 + n for n in range(5)},
    )
    first, second = swap("gx", 1, first), swap("gx", 0, second)
    level1 = [(6, 2, N1, 8, LN), (2, N1, 8, LN), (2, N1, 8, LN)]
    zs = (2, 5, 3, 16, 128)
    keep1, v1, react, diff2, matrix = call(
        inner_kernel, level1[:2] + [(16, 2, 16, 256), (3, 8, 128), (LN, 128)], [zs],
        (keep1, d1, counts), "inner", 8,
        aliases={0: 0}, cycles=10**7, dtypes=[F32] * 4 + [BF16],
    )
    message, keep1, _, _ = call(
        outer_kernel, [(2, 3, 8, 128)] + level1, [zs],
        (first, second, diff2, matrix, keep1, v1, d1), "outer", 8,
        aliases={4: 1, 5: 2, 6: 3},
    )
    gathered = everyone(message, "gx")
    tile, keep2, keep3 = call(
        middle_kernel,
        [(8, 128), (6, X2 + 2 * PAD, 8, 128), (6, X3 + 2 * PAD, 8, 128)],
        [(X2 + 2 * PAD, 8, 128), (X3 + 2 * PAD, 8, 128)] * 2 + [(2, 128, 128)],
        (gathered,), "middle", 8,
    )
    tiles = everyone(tile, "gy")
    (gradient,) = call(
        up_kernel,
        [(2, 16, 16, 256)],
        [
            (2, X4 + 16, 128), (128, 128), (10, 8, 128), (12, 8, 128), (8, 2, 8, LN),
            (2, N1, 8, LN), (2, N1, 8, LN), (2, NPL, 16, LN),
            (2, 5, 3, 16, 128),
        ],
        (tiles, keep2, keep3, keep0, keep1, react), "up", 12,
    )
    return gradient


def solution(mesh):
    in_specs = (P(None, None, "gx", "gy"), P(None, "gx", "gy"), P(), P(None, None, "gx", "gy"))
    out_specs = P(None, None, "gx", "gy")
    return jax.shard_map(
        per_device, mesh=mesh, in_specs=in_specs, out_specs=out_specs, check_vma=False
    )
```

time: 899 us -> 71.1 us (0.08)
  the two profiles are of different devices: /device:TPU:134 before, /device:TPU:1 now
where the time goes in v1:
time: 71.1 us; the launch traced here: 70.8 us
  blocking collectives  35.6 us (50%)
  starting transfers between devices  18 us (25%)
  Pallas kernels  14.7 us (21%)
  waiting for transfers between devices  1.43 us (2%)
  local copies, waits for them, and re-layouts  0.8 us (1%)
    all_to_all x2, blocking collectives, everyone(): return lax.all_to_all(copies, axis, split_axis=0, concat_axis=0, tiled=True)  35.6 us
    ppermute x8, starting transfers between devices, swap(): return lax.ppermute(block, axis, pairs + [(j, i) for i, j in pairs])  18 us
    pallas_call x10, Pallas kernels, call(): pl.pallas_call(kernel, out_shape=[jax.ShapeDtypeStruct(o, d) for o, d in...  14.7 us
    ppermute x8, waiting for transfers between devices, swap(): return lax.ppermute(block, axis, pairs + [(j, i) for i, j in pairs])  1.43 us
  transfers between devices with their start and end apart: 8, of which 1 were waited for; matrix products, arithmetic and copies ran while one was open for 0% of the time, Pallas kernels for 6%

profile of v1, /device:TPU:1, one launch (start us, length us, event | category | flops | bytes accessed | tf_op | source)
XLA Modules:
  0.0 70.8 jit_solution(2280830824295980026)
XLA Ops:
  0.0 0.0 copy-start.1
  0.0 0.0 copy-start.2
  0.0 0.0 copy-start.3
  0.0 0.7 %copy-done.3 = f32[2,8]{1,0:T(2,128)S(1)} copy-done((f32[2,8]{1,0:T(2,128)S(1)}, f32[2,8]{1,0:T(2,128)}, u32[]{:S(2)}) %copy-start.3) | copy-done | bytes 88
  0.8 0.6 table.1.table_in
  1.3 0.0 copy-done.1
  1.3 0.0 copy-done.2
  1.3 0.3 turn.1
  1.7 4.9 %collective-permute-start.2 = (f32[8,3,16,128]{3,2,1,0:T(8,128)S(1)}, f32[8,3,16,128]{3,2,1,0:T(8,128)S(1)}, u32[]{:S(2)}, u32[]{:S(2)}) collective-permute-start(f32[8,3,16,128]{3,2,1,0:T(8,128)S(1)} %get-tuple-element.38), channel_id=1, source_target_pairs={{1,2},{3,4},{5,6},{7,8},{9,10},{11,12},{13,14},{2,1},{4,3},{6,5},{... | collective-permute-start | bytes 589832 | tf_op jit(solution)/shard_map/ppermute | solution.py:685
  6.6 0.1 collective-permute-start.3
  6.7 0.7 collective-permute-start
  7.4 3.7 %collective-permute-start.1 = (f32[10,16,256]{2,1,0:T(8,128)S(1)}, f32[10,16,256]{2,1,0:T(8,128)S(1)}, u32[]{:S(2)}, u32[]{:S(2)}) collective-permute-start(f32[10,16,256]{2,1,0:T(8,128)S(1)} %get-tuple-element.37), channel_id=1, source_target_pairs={{0,16},{32,48},{64,80},{96,112},{128,144},{160,176},{192,208},{224... | collective-permute-start | bytes 491528 | tf_op jit(solution)/shard_map/ppermute | solution.py:685
  11.2 0.0 collective-permute-done.2.across
  11.2 0.0 collective-permute-done.3.inside
  11.2 0.1 edge.1
  11.3 0.7 collective-permute-start.4
  12.0 3.5 %collective-permute-start.5 = (f32[10,16,128]{2,1,0:T(8,128)S(1)}, f32[10,16,128]{2,1,0:T(8,128)S(1)}, u32[]{:S(2)}, u32[]{:S(2)}) collective-permute-start(f32[10,16,128]{2,1,0:T(8,128)S(1)} %get-tuple-element.41), channel_id=1, source_target_pairs={{0,16},{32,48},{64,80},{96,112},{128,144},{160,176},{192,208},{224... | collective-permute-start | bytes 245768 | tf_op jit(solution)/shard_map/ppermute | solution.py:685
  15.4 3.2 %own.1 = (f32[6,2,24,16,384]{4,3,2,1,0:T(8,128)S(1)}, f32[6,2,20,8,384]{4,3,2,1,0:T(8,128)S(1)}, f32[2,24,16,384]{3,2,1,0:T(8,128)S(1)}, f32[2,24,16,384]{3,2,1,0:T(8,128)S(1)}, f32[2,20,8,384]{3,2,1,0:T(8,128)S(1)}) custom-call(f32[16,128]{1,0:T(8,128)S(1)} %get-tuple-element.34.table, f32[16,3,16,256]{3,2,1,0:T(8,128)S(1)} %get-tuple-element.35.planes.own, ...), custom_call_target="tpu_custom_call" | custom-call | flops 10000000 | tf_op jit(solution)/shard_map/own/pallas_call | solution.py:668
  18.6 0.0 collective-permute-done.mfirst
  18.6 0.0 collective-permute-done.1.msecond
  18.6 0.0 collective-permute-done.4.sfirst
  18.6 0.0 collective-permute-done.5.ssecond
  18.6 0.0 copy-start
  18.6 2.0 %near.1 = (f32[9,8,384]{2,1,0:T(8,128)S(1)}, f32[9,8,384]{2,1,0:T(8,128)S(1)}, f32[6,2,24,16,384]{4,3,2,1,0:T(8,128)S(1)}, f32[6,2,20,8,384]{4,3,2,1,0:T(8,128)S...) custom-call(f32[16,128]{1,0:T(8,128)S(1)} %get-tuple-element.34.tabl, ...), custom_call_target="tpu_custom_call", output_to_operand_aliasing={{2}: (5, {}), {3}: (6, {}), {4}: (7, {}), {5}: (8, {}), {6}... | custom-call | tf_op jit(solution)/shard_map/near/pallas_call | solution.py:668
  20.7 0.7 collective-permute-start.6
  21.4 3.7 %collective-permute-start.7 = (f32[9,8,384]{2,1,0:T(8,128)S(1)}, f32[9,8,384]{2,1,0:T(8,128)S(1)}, u32[]{:S(2)}, u32[]{:S(2)}) collective-permute-start(f32[9,8,384]{2,1,0:T(8,128)S(1)} %get-tuple-element.49), channel_id=1, source_target_pairs={{0,16},{32,48},{64,80},{96,112},{128,144},{160,176},{192,208},{224... | collective-permute-start | bytes 331784 | tf_op jit(solution)/shard_map/ppermute | solution.py:685
  25.1 0.0 copy-done
  25.1 0.7 inner.1
  25.8 0.0 collective-permute-done.6.first
  25.8 1.4 %collective-permute-done.7.second = f32[9,8,384]{2,1,0:T(8,128)S(1)} collective-permute-done((f32[9,8,384]{2,1,0:T(8,128)S(1)}, f32[9,8,384]{2,1,0:T(8,128)S(1)}, u32[]{:S(2)}, u32[]{:S(2)}) %collective-permute-start.7) | collective-permute-done | bytes 110624 | tf_op jit(solution)/shard_map/ppermute | solution.py:685
  27.3 0.9 %outer.1 = (f32[2,3,8,128]{3,2,1,0:T(8,128)S(1)}, f32[6,2,20,8,384]{4,3,2,1,0:T(8,128)S(1)}, f32[2,20,8,384]{3,2,1,0:T(8,128)S(1)}, f32[2,20,8,384]{3,2,1,0:T(8,128)S(1)}) custom-call(f32[9,8,384]{2,1,0:T(8,128)S(1)} %collective-permute-done.6.first, ...), custom_call_target="tpu_custom_call", output_to_operand_aliasing={{1}: (4, {}), {2}: (5, {}), {3}: (6, {})} | custom-call | tf_op jit(solution)/shard_map/outer/pallas_call | solution.py:668
  28.2 15.2 %all_to_all.10.gathered = f32[16,2,3,8,128]{4,3,2,1,0:T(8,128)S(1)} all-to-all(f32[16,2,3,8,128]{4,3,2,1,0:T(8,128)S(1)} %broadcast_in_dim.4), channel_id=1, replica_groups=mesh['gx'=16,'gy'=16] {'gx'}, dimensions={0} | all-to-all | bytes 786432 | tf_op jit(solution)/shard_map/all_to_all | solution.py:691
  43.3 2.1 %middle.1 = (f32[8,128]{1,0:T(8,128)S(1)}, f32[6,72,8,128]{3,2,1,0:T(8,128)S(1)}, f32[6,40,8,128]{3,2,1,0:T(8,128)S(1)}) custom-call(f32[16,2,3,8,128]{4,3,2,1,0:T(8,128)S(1)} %all_to_all.10.gathered), custom_call_target="tpu_custom_call" | custom-call | tf_op jit(solution)/shard_map/middle/pallas_call | solution.py:668
  45.5 20.5 %all_to_all.11.tiles = f32[16,8,128]{2,1,0:T(8,128)S(1)} all-to-all(f32[16,8,128]{2,1,0:T(8,128)S(1)} %broadcast_in_dim.5), channel_id=1, replica_groups=mesh['gx'=16,'gy'=16] {'gy'}, dimensions={0} | all-to-all | bytes 131072 | tf_op jit(solution)/shard_map/all_to_all | solution.py:691
  66.0 4.8 %up.1 = f32[2,16,16,256]{3,2,1,0:T(8,128)} custom-call(f32[16,8,128]{2,1,0:T(8,128)S(1)} %all_to_all.11.tiles, f32[6,72,8,128]{3,2,1,0:T(8,128)S(1)} %get-tuple-element.58.keep2, f32[6,40,8,128]{3,2,1,0:T(8,128)S(1)} %get-tuple-element.59.keep3, f32[6,2,24,16,384]{4,3,2,1,0:T(8,128)S(1)} %get-tuple-element.60.keep0, ...), custom_call_target="tpu_custom_call" | custom-call | tf_op jit(solution)/shard_map/up/pallas_call | solution.py:668
  (3 shorter events, 0.1 us)
Async XLA Ops:
  0.0 1.3 %copy-start.1 = (f32[2,16,16,256]{3,2,1,0:T(8,128)S(1)}, f32[2,16,16,256]{3,2,1,0:T(8,128)}, u32[]{:S(2)}) copy-start(f32[2,16,16,256]{3,2,1,0:T(8,128)} %cot.1) | copy-start | bytes 1572868
  0.0 1.3 %copy-start.2 = (s32[16,16,256]{2,1,0:T(8,128)S(1)}, s32[16,16,256]{2,1,0:T(8,128)}, u32[]{:S(2)}) copy-start(s32[16,16,256]{2,1,0:T(8,128)} %cls.1) | copy-start | bytes 786436
  0.0 0.8 %copy-start.3 = (f32[2,8]{1,0:T(2,128)S(1)}, f32[2,8]{1,0:T(2,128)}, u32[]{:S(2)}) copy-start(f32[2,8]{1,0:T(2,128)} %diff_ref.1) | copy-start | bytes 196
  1.7 9.5 %collective-permute-start.2 = (f32[8,3,16,128]{3,2,1,0:T(8,128)S(1)}, f32[8,3,16,128]{3,2,1,0:T(8,128)S(1)}, u32[]{:S(2)}, u32[]{:S(2)}) collective-permute-start(f32[8,3,16,128]{3,2,1,0:T(8,128)S(1)} %get-tuple-element.38), channel_id=1, source_target_pairs={{1,2},{3,4},{5,6},{7,8},{9,10},{11,12},{13,14},{2,1},{4,3},{6,5},{... | collective-permute-start | bytes 589832 | tf_op jit(solution)/shard_map/ppermute | solution.py:685
  6.6 4.6 %collective-permute-start.3 = (f32[8,3,16,128]{3,2,1,0:T(8,128)S(1)}, f32[8,3,16,128]{3,2,1,0:T(8,128)S(1)}, u32[]{:S(2)}, u32[]{:S(2)}) collective-permute-start(f32[8,3,16,128]{3,2,1,0:T(8,128)S(1)} %get-tuple-element.39), channel_id=1, source_target_pairs={{0,1},{2,3},{4,5},{6,7},{8,9},{10,11},{12,13},{14,15},{1,0},{3,2},... | collective-permute-start | bytes 589832 | tf_op jit(solution)/shard_map/ppermute | solution.py:685
  6.7 11.8 %collective-permute-start = (f32[10,16,256]{2,1,0:T(8,128)S(1)}, f32[10,16,256]{2,1,0:T(8,128)S(1)}, u32[]{:S(2)}, u32[]{:S(2)}) collective-permute-start(f32[10,16,256]{2,1,0:T(8,128)S(1)} %get-tuple-element.36), channel_id=1, source_target_pairs={{16,32},{48,64},{80,96},{112,128},{144,160},{176,192},{208,224},{3... | collective-permute-start | bytes 491528 | tf_op jit(solution)/shard_map/ppermute | solution.py:685
  7.4 11.2 %collective-permute-start.1 = (f32[10,16,256]{2,1,0:T(8,128)S(1)}, f32[10,16,256]{2,1,0:T(8,128)S(1)}, u32[]{:S(2)}, u32[]{:S(2)}) collective-permute-start(f32[10,16,256]{2,1,0:T(8,128)S(1)} %get-tuple-element.37), channel_id=1, source_target_pairs={{0,16},{32,48},{64,80},{96,112},{128,144},{160,176},{192,208},{224... | collective-permute-start | bytes 491528 | tf_op jit(solution)/shard_map/ppermute | solution.py:685
  11.3 7.3 %collective-permute-start.4 = (f32[10,16,128]{2,1,0:T(8,128)S(1)}, f32[10,16,128]{2,1,0:T(8,128)S(1)}, u32[]{:S(2)}, u32[]{:S(2)}) collective-permute-start(f32[10,16,128]{2,1,0:T(8,128)S(1)} %get-tuple-element.40), channel_id=1, source_target_pairs={{16,32},{48,64},{80,96},{112,128},{144,160},{176,192},{208,224},{3... | collective-permute-start | bytes 245768 | tf_op jit(solution)/shard_map/ppermute | solution.py:685
  12.0 6.7 %collective-permute-start.5 = (f32[10,16,128]{2,1,0:T(8,128)S(1)}, f32[10,16,128]{2,1,0:T(8,128)S(1)}, u32[]{:S(2)}, u32[]{:S(2)}) collective-permute-start(f32[10,16,128]{2,1,0:T(8,128)S(1)} %get-tuple-element.41), channel_id=1, source_target_pairs={{0,16},{32,48},{64,80},{96,112},{128,144},{160,176},{192,208},{224... | collective-permute-start | bytes 245768 | tf_op jit(solution)/shard_map/ppermute | solution.py:685
  18.6 6.5 %copy-start = (s32[2,16,16,256]{3,2,1,0:T(8,128)S(1)}, s32[2,16,16,256]{3,2,1,0:T(8,128)}, u32[]{:S(2)}) copy-start(s32[2,16,16,256]{3,2,1,0:T(8,128)} %counts.1) | copy-start | bytes 1572868
  20.7 5.1 %collective-permute-start.6 = (f32[9,8,384]{2,1,0:T(8,128)S(1)}, f32[9,8,384]{2,1,0:T(8,128)S(1)}, u32[]{:S(2)}, u32[]{:S(2)}) collective-permute-start(f32[9,8,384]{2,1,0:T(8,128)S(1)} %get-tuple-element.48), channel_id=1, source_target_pairs={{16,32},{48,64},{80,96},{112,128},{144,160},{176,192},{208,224},{3... | collective-permute-start | bytes 331784 | tf_op jit(solution)/shard_map/ppermute | solution.py:685
  21.4 5.9 %collective-permute-start.7 = (f32[9,8,384]{2,1,0:T(8,128)S(1)}, f32[9,8,384]{2,1,0:T(8,128)S(1)}, u32[]{:S(2)}, u32[]{:S(2)}) collective-permute-start(f32[9,8,384]{2,1,0:T(8,128)S(1)} %get-tuple-element.49), channel_id=1, source_target_pairs={{0,16},{32,48},{64,80},{96,112},{128,144},{160,176},{192,208},{224... | collective-permute-start | bytes 331784 | tf_op jit(solution)/shard_map/ppermute | solution.py:685

commit v2 on v1

--- a/solution.py
+++ b/solution.py
@@ -39,6 +39,18 @@
     return pl.reciprocal(x, approx=True)
 
 
+def z_up(value, step):
+    if step:
+        return shift_up(value, step, 0)
+    return jnp.concatenate([shift_up(value[8:], 1, 0), value[:8]], axis=0)
+
+
+def z_down(value, step):
+    if step:
+        return shift_down(value, step, 0)
+    return jnp.concatenate([value[8:], shift_down(value[:8], 1, 0)], axis=0)
+
+
 def harm(a, b):
     return a * b * reciprocal(a + b)
 
@@ -46,18 +58,18 @@
 def residual(u, b, fx, fxn, wy, wz, sy, sz):
     fy = wy * (u - shift_up(u, sy, 1))
     mu = u + (fx - fxn) + (fy - shift_down(fy, sy, 1))
-    fz = wz * (u - shift_up(u, sz, 0))
-    return b - (mu + (fz - shift_down(fz, sz, 0)))
+    fz = wz * (u - z_up(u, sz))
+    return b - (mu + (fz - z_down(fz, sz)))
 
 
 def residual_short(u, b, fx, fxn, wy, wz, sy, sz):
     fy = wy * (u - shift_up(u, sy, 1)) - shift_down(wy, sy, 1) * (shift_down(u, sy, 1) - u)
-    fz = wz * (u - shift_up(u, sz, 0)) - shift_down(wz, sz, 0) * (shift_down(u, sz, 0) - u)
+    fz = wz * (u - z_up(u, sz)) - z_down(wz, sz) * (z_down(u, sz) - u)
     return b - (u + (fx - fxn) + (fy + fz))
 
 
 def diagonal(wx, wxn, wy, wz, sy, sz):
-    return 1.0 + (wx + wxn) + (wy + shift_down(wy, sy, 1)) + (wz + shift_down(wz, sz, 0))
+    return 1.0 + (wx + wxn) + (wy + shift_down(wy, sy, 1)) + (wz + z_down(wz, sz))
 
 
 def pair_lanes(value, half):
@@ -71,30 +83,6 @@
     total = value + shift_down(value, half, 0)
     first = (iota(value.shape, 0) // half) % 2 == 0
     return jnp.where(first, total, shift_up(total, half, 0))
-
-
-def split_store(ref, value):
-    for k in range(value.shape[1] // 128):
-        ref[k] = value[:, 128 * k : 128 * (k + 1)]
-
-
-def sum_depth(ref, value):
-    rows = value.shape[0]
-    split_store(ref, value)
-    parts = [
-        ref[k, pl.ds(0, rows // 2, stride=2), :] + ref[k, pl.ds(1, rows // 2, stride=2), :]
-        for k in range(value.shape[1] // 128)
-    ]
-    return jnp.concatenate(parts, axis=1)
-
-
-def spread_depth(ref, value):
-    rows = value.shape[0]
-    for k in range(3):
-        part = value[:, 128 * k : 128 * (k + 1)]
-        ref[k, pl.ds(0, rows, stride=2), :] = part
-        ref[k, pl.ds(1, rows, stride=2), :] = part
-    return jnp.concatenate([ref[k] for k in range(3)], axis=1)
 
 
 def pick_lanes(value, lanes):
@@ -120,7 +108,7 @@
         after = d[p + 1]
         siden = factor_x(p + 1) * harm(after, here)
         y = my * harm(here, shift_up(here, sy, 1))
-        z = mz * harm(here, shift_up(here, sz, 0))
+        z = mz * harm(here, z_up(here, sz))
         wx[p], wy[p], wz[p] = side, y, z
         value = RELAX * reciprocal(diagonal(side, siden, y, z, sy, sz))
         inv[p] = value
@@ -155,7 +143,8 @@
         for k in range(8):
             pair = []
             for x in (k, k + 8):
-                pair.append(cls[:, x, :].astype(F32) if f == 2 else cot[f, :, x, :])
+                halves = [cls[:, n, x, :] if f == 2 else cot[f, :, n, x, :] for n in range(2)]
+                pair.append(jnp.concatenate(halves, axis=0).astype(F32))
                 own[x, f] = pair[-1]
             a, b = pair
             to_left = jnp.where(left_half, a[:, :128], pltpu.roll(b[:, :128], HY, 1))
@@ -187,7 +176,7 @@
     cut_strips(edge, first, second)
 
 
-def fine_tools(table, keep0, keep1, d0, v0, d1, zs):
+def fine_tools(table, keep0, keep1, d0, v0, d1):
     gx = lax.axis_index("gx")
     gy = lax.axis_index("gy")
     nx = 16 * lax.axis_size("gx")
@@ -255,7 +244,7 @@
             for s in range(2):
                 face_weights(
                     d.at[s], keep.at[1, s], keep.at[2, s], keep.at[3, s], keep.at[4, s],
-                    keep.at[0, s], v.at[s], start, size, factor_x, my, mz, step, 1,
+                    keep.at[0, s], v.at[s], start, size, factor_x, my, mz, step, 0 if step == 1 else 1,
                 )
 
         return body
@@ -263,7 +252,7 @@
     def planes(keep, u, s, start, size, step):
         return stencil(
             u.at[s], keep.at[0, s], keep.at[1, s], keep.at[2, s], keep.at[3, s],
-            start, size, step, 1,
+            start, size, step, 0 if step == 1 else 1,
         )
 
     def smooth(lo, hi, size, keep, v, step):
@@ -285,8 +274,8 @@
             for s in range(2):
                 res = [r for _, _, r in planes(keep0, u0, s, 2 * start - 8, 2 * size, 1)]
                 for i in range(size):
-                    total = pair_lanes(res[2 * i] + res[2 * i + 1], 1)
-                    b1[s, start + i] = 0.125 * sum_depth(zs.at[s, i], total)
+                    total = res[2 * i] + res[2 * i + 1]
+                    b1[s, start + i] = 0.125 * pair_lanes(total[:8] + total[8:], 1)
 
         return body
 
@@ -295,8 +284,8 @@
             for i in range(size):
                 for s in range(2):
                     p = 2 * (start + i) - 8
-                    total = pair_lanes(d0[s, p] + d0[s, p + 1], 1)
-                    d1[s, start + i] = 0.125 * sum_depth(zs.at[s, i], total)
+                    total = d0[s, p] + d0[s, p + 1]
+                    d1[s, start + i] = 0.125 * pair_lanes(total[:8] + total[8:], 1)
 
         blocks(lo, hi, size, body)
 
@@ -308,9 +297,9 @@
 COARSER = 0.5 * STEP
 
 
-def own_kernel(table, own, edge, keep0, keep1, d0, v0, d1, zs):
+def own_kernel(table, own, edge, keep0, keep1, d0, v0, d1):
     assemble_own, _, weigh, smooth, restrict, coarse_diff, _ = fine_tools(
-        table, keep0, keep1, d0, v0, d1, zs
+        table, keep0, keep1, d0, v0, d1
     )
     assemble_own(own, edge, 4)
     weigh(5, 19, 7, 16, 1, FINE, d0, keep0, v0)
@@ -322,9 +311,8 @@
 def near_kernel(
     table, mfirst, msecond, sfirst, ssecond, keep0_in, keep1_in, d0_in, v0_in, d1_in,
     first, second, keep0, keep1, d0, v0, d1,
-    zs,
 ):
-    _, at, _, _, _, _, _ = fine_tools(table, keep0, keep1, d0, v0, d1, zs)
+    _, at, _, _, _, _, _ = fine_tools(table, keep0, keep1, d0, v0, d1)
     assemble_strip, weigher, smoother, restricter = at
     weigh = weigher(4, 16, 1, FINE, d0, keep0, v0)
     smooth = smoother(4, keep0, v0, 1)
@@ -371,7 +359,7 @@
     lane = iota((8, 128), 1)
     halved = []
     for n in range(4):
-        part = zs.at[0, n, 0]
+        part = zs.at[n]
         part[...] = whole[16 * n : 16 * (n + 1)]
         halved.append(part[pl.ds(0, 8, stride=2), :] + part[pl.ds(1, 8, stride=2), :])
     for k in range(3):
@@ -379,12 +367,13 @@
 
 
 def inner_kernel(keep1_in, d1, counts, keep1, v1, react, diff2, matrix, zs):
-    _, _, weigh, smooth, _, _, _ = fine_tools(None, keep1, keep1, None, None, d1, zs)
+    _, _, weigh, smooth, _, _, _ = fine_tools(None, keep1, keep1, None, None, d1)
     weigh(7, 13, 6, 8, 2, COARSER, d1, keep1, v1)
     smooth(8, 12, 4, keep1, v1, 2)
     for s in range(2):
         for x in range(16):
-            react[x, s] = REACT * (0.25 * counts[s, :, x, :].astype(F32))
+            halves = [counts[s, :, n, x, :] for n in range(2)]
+            react[x, s] = REACT * (0.25 * jnp.concatenate(halves, axis=0).astype(F32))
     matrix[...] = averaging((LN, 128), BF16)
     rows = [d1[s, 6 + 2 * n] + d1[s, 7 + 2 * n] for n in range(4) for s in range(2)]
     to_level2(rows, matrix[...], zs, diff2)
@@ -395,7 +384,7 @@
     message, keep1, v1, d1,
     zs,
 ):
-    _, _, weigh, smooth, _, _, planes = fine_tools(None, keep1, keep1, None, None, d1, zs)
+    _, _, weigh, smooth, _, _, planes = fine_tools(None, keep1, keep1, None, None, d1)
     gx = lax.axis_index("gx")
     last = lax.axis_size("gx") - 1
     odd = gx % 2 == 1
@@ -551,7 +540,7 @@
 def up_kernel(
     tiles, keep2, keep3, keep0, keep1, react,
     out,
-    c4, rep2, u3, u2, c2, p1, q1, q0, zs,
+    c4, rep2, u3, u2, c2, p1, q1, q0,
 ):
     gx = lax.axis_index("gx")
     gy = lax.axis_index("gy")
@@ -610,7 +599,7 @@
     def planes(keep, u, s, start, size, step):
         return stencil(
             u.at[s], keep.at[0, s], keep.at[1, s], keep.at[2, s], keep.at[3, s],
-            start, size, step, 1,
+            start, size, step, 0 if step == 1 else 1,
         )
 
     def smooth(lo, hi, size, keep, u, new, step):
@@ -630,14 +619,15 @@
     def corrected_sweep(n, carry):
         start = 3 + 6 * n
         for s in range(2):
-            spread = [spread_depth(zs.at[s, j], p1[s, 5 + 3 * n + j]) for j in range(4)]
+            spread = [p1[s, 5 + 3 * n + j] for j in range(4)]
+            spread = [jnp.concatenate([c, c], axis=0) for c in spread]
             u = [keep0[5, s, start - 1 + j] + spread[j // 2] for j in range(8)]
             fx = keep0[1, s, start] * (u[1] - u[0])
             for j in range(6):
                 p = start + j
                 fxn = keep0[1, s, p + 1] * (u[j + 2] - u[j + 1])
                 r = residual(
-                    u[j + 1], keep0[0, s, p], fx, fxn, keep0[2, s, p], keep0[3, s, p], 1, 1
+                    u[j + 1], keep0[0, s, p], fx, fxn, keep0[2, s, p], keep0[3, s, p], 1, 0
                 )
                 q0[s, p] = u[j + 1] + keep0[4, s, p] * r
                 fx = fxn
@@ -654,8 +644,9 @@
             x = start + j - HX
             a0, a1 = adj[0][j], adj[1][j]
             total = a0 + a1
-            out[0, :, x, :] = a0 - react[x, 1] * total
-            out[1, :, x, :] = a1 - react[x, 0] * total
+            for s, value in enumerate((a0 - react[x, 1] * total, a1 - react[x, 0] * total)):
+                out[s, :, 0, x, :] = value[:8]
+                out[s, :, 1, x, :] = value[8:]
 
     blocks(4, 20, 4, last)
 
@@ -692,6 +683,9 @@
 
 
 def per_device(counts, classes, diffusivity, cotangent):
+    shape = cotangent.shape
+    counts, cotangent = (a.reshape(2, 8, 2, 16, 256) for a in (counts, cotangent))
+    classes = classes.reshape(8, 2, 16, 256)
     (table,) = call(table_kernel, [(16, 128)], [], (diffusivity,), "table", 8, "s", cycles=10**9)
     own, across, inside, table = call(
         turn_kernel,
@@ -709,18 +703,17 @@
     sfirst, ssecond = swap("gx", 1, sfirst), swap("gx", 0, ssecond)
     fine = [(6, 2, NPL, 16, LN), (6, 2, N1, 8, LN)]
     fine += [(2, NPL, 16, LN)] * 2 + [(2, N1, 8, LN)]
-    zs = (2, 4, 3, 16, 128)
-    kept = call(own_kernel, fine, [zs], (table, own, edge), "own", 8, cycles=10**7)
+    kept = call(own_kernel, fine, [], (table, own, edge), "own", 8, cycles=10**7)
     strip = (9, 8, LN)
     first, second, keep0, keep1, _, _, d1 = call(
         near_kernel,
-        [strip, strip] + fine, [zs],
+        [strip, strip] + fine, [],
         (table, mfirst, msecond, sfirst, ssecond, *kept), "near", 8,
         aliases={5 + n: 2 + n for n in range(5)},
     )
     first, second = swap("gx", 1, first), swap("gx", 0, second)
     level1 = [(6, 2, N1, 8, LN), (2, N1, 8, LN), (2, N1, 8, LN)]
-    zs = (2, 5, 3, 16, 128)
+    zs = (4, 16, 128)
     keep1, v1, react, diff2, matrix = call(
         inner_kernel, level1[:2] + [(16, 2, 16, 256), (3, 8, 128), (LN, 128)], [zs],
         (keep1, d1, counts), "inner", 8,
@@ -741,15 +734,14 @@
     tiles = everyone(tile, "gy")
     (gradient,) = call(
         up_kernel,
-        [(2, 16, 16, 256)],
+        [(2, 8, 2, 16, 256)],
         [
             (2, X4 + 16, 128), (128, 128), (10, 8, 128), (12, 8, 128), (8, 2, 8, LN),
             (2, N1, 8, LN), (2, N1, 8, LN), (2, NPL, 16, LN),
-            (2, 5, 3, 16, 128),
         ],
         (tiles, keep2, keep3, keep0, keep1, react), "up", 12,
     )
-    return gradient
+    return gradient.reshape(shape)
 
 
 def solution(mesh):

time: 71.1 us -> 70.9 us (level)
  transfers between devices with their start and end apart: 8 -> 8, of which waited for: 1 -> 1; matrix products, arithmetic and copies ran while one was open for 0% -> 0% of each run, Pallas kernels for 6% -> 5%
where the time goes in v2:
time: 70.9 us; the launch traced here: 70.6 us
  blocking collectives  35.9 us (51%)
  starting transfers between devices  18 us (25%)
  Pallas kernels  14.2 us (20%)
  waiting for transfers between devices  1.58 us (2%)
  local copies, waits for them, and re-layouts  0.8 us (1%)
    all_to_all x2, blocking collectives, everyone(): return lax.all_to_all(copies, axis, split_axis=0, concat_axis=0, tiled=True)  35.9 us
    ppermute x8, starting transfers between devices, swap(): return lax.ppermute(block, axis, pairs + [(j, i) for i, j in pairs])  18 us
    pallas_call x10, Pallas kernels, call(): pl.pallas_call(kernel, out_shape=[jax.ShapeDtypeStruct(o, d) for o, d in...  14.2 us
    ppermute x8, waiting for transfers between devices, swap(): return lax.ppermute(block, axis, pairs + [(j, i) for i, j in pairs])  1.58 us
  transfers between devices with their start and end apart: 8, of which 1 were waited for; matrix products, arithmetic and copies ran while one was open for 0% of the time, Pallas kernels for 5%

profile of v2, /device:TPU:1, one launch (start us, length us, event | category | flops | bytes accessed | tf_op | source)
XLA Modules:
  0.0 70.6 jit_solution(9834421070986196979)
XLA Ops:
  0.0 0.0 copy-start.1
  0.0 0.0 copy-start.2
  0.0 0.0 copy-start.3
  0.0 0.7 %copy-done.3 = f32[2,8]{1,0:T(2,128)S(1)} copy-done((f32[2,8]{1,0:T(2,128)S(1)}, f32[2,8]{1,0:T(2,128)}, u32[]{:S(2)}) %copy-start.3) | copy-done | bytes 88
  0.8 0.6 table.1.table_in
  1.3 0.0 copy-done.1
  1.3 0.0 copy-done.2
  1.3 0.3 turn.1
  1.6 4.9 %collective-permute-start.2 = (f32[8,3,16,128]{3,2,1,0:T(8,128)S(1)}, f32[8,3,16,128]{3,2,1,0:T(8,128)S(1)}, u32[]{:S(2)}, u32[]{:S(2)}) collective-permute-start(f32[8,3,16,128]{3,2,1,0:T(8,128)S(1)} %get-tuple-element.38), channel_id=1, source_target_pairs={{1,2},{3,4},{5,6},{7,8},{9,10},{11,12},{13,14},{2,1},{4,3},{6,5},{... | collective-permute-start | bytes 589832 | tf_op jit(solution)/shard_map/ppermute | solution.py:676
  6.6 0.1 collective-permute-start.3
  6.7 0.7 collective-permute-start
  7.4 3.7 %collective-permute-start.1 = (f32[10,16,256]{2,1,0:T(8,128)S(1)}, f32[10,16,256]{2,1,0:T(8,128)S(1)}, u32[]{:S(2)}, u32[]{:S(2)}) collective-permute-start(f32[10,16,256]{2,1,0:T(8,128)S(1)} %get-tuple-element.37), channel_id=1, source_target_pairs={{0,16},{32,48},{64,80},{96,112},{128,144},{160,176},{192,208},{224... | collective-permute-start | bytes 491528 | tf_op jit(solution)/shard_map/ppermute | solution.py:676
  11.2 0.0 collective-permute-done.2.across
  11.2 0.0 collective-permute-done.3.inside
  11.2 0.1 edge.1
  11.3 0.7 collective-permute-start.4
  12.0 3.5 %collective-permute-start.5 = (f32[10,16,128]{2,1,0:T(8,128)S(1)}, f32[10,16,128]{2,1,0:T(8,128)S(1)}, u32[]{:S(2)}, u32[]{:S(2)}) collective-permute-start(f32[10,16,128]{2,1,0:T(8,128)S(1)} %get-tuple-element.41), channel_id=1, source_target_pairs={{0,16},{32,48},{64,80},{96,112},{128,144},{160,176},{192,208},{224... | collective-permute-start | bytes 245768 | tf_op jit(solution)/shard_map/ppermute | solution.py:676
  15.4 2.9 %own.1 = (f32[6,2,24,16,384]{4,3,2,1,0:T(8,128)S(1)}, f32[6,2,20,8,384]{4,3,2,1,0:T(8,128)S(1)}, f32[2,24,16,384]{3,2,1,0:T(8,128)S(1)}, f32[2,24,16,384]{3,2,1,0:T(8,128)S(1)}, f32[2,20,8,384]{3,2,1,0:T(8,128)S(1)}) custom-call(f32[16,128]{1,0:T(8,128)S(1)} %get-tuple-element.34.table, f32[16,3,16,256]{3,2,1,0:T(8,128)S(1)} %get-tuple-element.35.planes.own, ...), custom_call_target="tpu_custom_call" | custom-call | flops 10000000 | tf_op jit(solution)/shard_map/own/pallas_call | solution.py:659
  18.3 0.0 collective-permute-done.mfirst
  18.3 0.0 collective-permute-done.1.msecond
  18.3 0.0 collective-permute-done.4.sfirst
  18.3 0.0 collective-permute-done.5.ssecond
  18.3 0.0 copy-start
  18.4 1.9 %near.1 = (f32[9,8,384]{2,1,0:T(8,128)S(1)}, f32[9,8,384]{2,1,0:T(8,128)S(1)}, f32[6,2,24,16,384]{4,3,2,1,0:T(8,128)S(1)}, f32[6,2,20,8,384]{4,3,2,1,0:T(8,128)S...) custom-call(f32[16,128]{1,0:T(8,128)S(1)} %get-tuple-element.34.tabl, ...), custom_call_target="tpu_custom_call", output_to_operand_aliasing={{2}: (5, {}), {3}: (6, {}), {4}: (7, {}), {5}: (8, {}), {6}... | custom-call | tf_op jit(solution)/shard_map/near/pallas_call | solution.py:659
  20.3 0.7 collective-permute-start.6
  21.0 3.7 %collective-permute-start.7 = (f32[9,8,384]{2,1,0:T(8,128)S(1)}, f32[9,8,384]{2,1,0:T(8,128)S(1)}, u32[]{:S(2)}, u32[]{:S(2)}) collective-permute-start(f32[9,8,384]{2,1,0:T(8,128)S(1)} %get-tuple-element.49), channel_id=1, source_target_pairs={{0,16},{32,48},{64,80},{96,112},{128,144},{160,176},{192,208},{224... | collective-permute-start | bytes 331784 | tf_op jit(solution)/shard_map/ppermute | solution.py:676
  24.7 0.0 copy-done
  24.7 0.6 inner.1
  25.3 0.0 collective-permute-done.6.first
  25.3 1.6 %collective-permute-done.7.second = f32[9,8,384]{2,1,0:T(8,128)S(1)} collective-permute-done((f32[9,8,384]{2,1,0:T(8,128)S(1)}, f32[9,8,384]{2,1,0:T(8,128)S(1)}, u32[]{:S(2)}, u32[]{:S(2)}) %collective-permute-start.7) | collective-permute-done | bytes 110624 | tf_op jit(solution)/shard_map/ppermute | solution.py:676
  26.9 0.9 %outer.1 = (f32[2,3,8,128]{3,2,1,0:T(8,128)S(1)}, f32[6,2,20,8,384]{4,3,2,1,0:T(8,128)S(1)}, f32[2,20,8,384]{3,2,1,0:T(8,128)S(1)}, f32[2,20,8,384]{3,2,1,0:T(8,128)S(1)}) custom-call(f32[9,8,384]{2,1,0:T(8,128)S(1)} %collective-permute-done.6.first, ...), custom_call_target="tpu_custom_call", output_to_operand_aliasing={{1}: (4, {}), {2}: (5, {}), {3}: (6, {})} | custom-call | tf_op jit(solution)/shard_map/outer/pallas_call | solution.py:659
  27.8 15.4 %all_to_all.10.gathered = f32[16,2,3,8,128]{4,3,2,1,0:T(8,128)S(1)} all-to-all(f32[16,2,3,8,128]{4,3,2,1,0:T(8,128)S(1)} %broadcast_in_dim.4), channel_id=1, replica_groups=mesh['gx'=16,'gy'=16] {'gx'}, dimensions={0} | all-to-all | bytes 786432 | tf_op jit(solution)/shard_map/all_to_all | solution.py:682
  43.2 2.1 %middle.1 = (f32[8,128]{1,0:T(8,128)S(1)}, f32[6,72,8,128]{3,2,1,0:T(8,128)S(1)}, f32[6,40,8,128]{3,2,1,0:T(8,128)S(1)}) custom-call(f32[16,2,3,8,128]{4,3,2,1,0:T(8,128)S(1)} %all_to_all.10.gathered), custom_call_target="tpu_custom_call" | custom-call | tf_op jit(solution)/shard_map/middle/pallas_call | solution.py:659
  45.4 20.5 %all_to_all.11.tiles = f32[16,8,128]{2,1,0:T(8,128)S(1)} all-to-all(f32[16,8,128]{2,1,0:T(8,128)S(1)} %broadcast_in_dim.5), channel_id=1, replica_groups=mesh['gx'=16,'gy'=16] {'gy'}, dimensions={0} | all-to-all | bytes 131072 | tf_op jit(solution)/shard_map/all_to_all | solution.py:682
  65.9 4.8 %up.1 = f32[2,8,2,16,256]{4,3,2,1,0:T(8,128)} custom-call(f32[16,8,128]{2,1,0:T(8,128)S(1)} %all_to_all.11.tiles, f32[6,72,8,128]{3,2,1,0:T(8,128)S(1)} %get-tuple-element.58.keep2, f32[6,40,8,128]{3,2,1,0:T(8,128)S(1)} %get-tuple-element.59.keep3, f32[6,2,24,16,384]{4,3,2,1,0:T(8,128)S(1)} %get-tuple-element.60.keep0, ...), custom_call_target="tpu_custom_call" | custom-call | tf_op jit(solution)/shard_map/up/pallas_call | solution.py:659
  (3 shorter events, 0.1 us)
Async XLA Ops:
  0.0 1.3 %copy-start.1 = (f32[2,16,16,256]{3,2,1,0:T(8,128)S(1)}, f32[2,16,16,256]{3,2,1,0:T(8,128)}, u32[]{:S(2)}) copy-start(f32[2,16,16,256]{3,2,1,0:T(8,128)} %param.7) | copy-start | bytes 1572868
  0.0 1.3 %copy-start.2 = (s32[16,16,256]{2,1,0:T(8,128)S(1)}, s32[16,16,256]{2,1,0:T(8,128)}, u32[]{:S(2)}) copy-start(s32[16,16,256]{2,1,0:T(8,128)} %param.5) | copy-start | bytes 786436
  0.0 0.8 %copy-start.3 = (f32[2,8]{1,0:T(2,128)S(1)}, f32[2,8]{1,0:T(2,128)}, u32[]{:S(2)}) copy-start(f32[2,8]{1,0:T(2,128)} %diff_ref.1) | copy-start | bytes 196
  1.6 9.5 %collective-permute-start.2 = (f32[8,3,16,128]{3,2,1,0:T(8,128)S(1)}, f32[8,3,16,128]{3,2,1,0:T(8,128)S(1)}, u32[]{:S(2)}, u32[]{:S(2)}) collective-permute-start(f32[8,3,16,128]{3,2,1,0:T(8,128)S(1)} %get-tuple-element.38), channel_id=1, source_target_pairs={{1,2},{3,4},{5,6},{7,8},{9,10},{11,12},{13,14},{2,1},{4,3},{6,5},{... | collective-permute-start | bytes 589832 | tf_op jit(solution)/shard_map/ppermute | solution.py:676
  6.6 4.6 %collective-permute-start.3 = (f32[8,3,16,128]{3,2,1,0:T(8,128)S(1)}, f32[8,3,16,128]{3,2,1,0:T(8,128)S(1)}, u32[]{:S(2)}, u32[]{:S(2)}) collective-permute-start(f32[8,3,16,128]{3,2,1,0:T(8,128)S(1)} %get-tuple-element.39), channel_id=1, source_target_pairs={{0,1},{2,3},{4,5},{6,7},{8,9},{10,11},{12,13},{14,15},{1,0},{3,2},... | collective-permute-start | bytes 589832 | tf_op jit(solution)/shard_map/ppermute | solution.py:676
  6.7 11.6 %collective-permute-start = (f32[10,16,256]{2,1,0:T(8,128)S(1)}, f32[10,16,256]{2,1,0:T(8,128)S(1)}, u32[]{:S(2)}, u32[]{:S(2)}) collective-permute-start(f32[10,16,256]{2,1,0:T(8,128)S(1)} %get-tuple-element.36), channel_id=1, source_target_pairs={{16,32},{48,64},{80,96},{112,128},{144,160},{176,192},{208,224},{3... | collective-permute-start | bytes 491528 | tf_op jit(solution)/shard_map/ppermute | solution.py:676
  7.4 10.9 %collective-permute-start.1 = (f32[10,16,256]{2,1,0:T(8,128)S(1)}, f32[10,16,256]{2,1,0:T(8,128)S(1)}, u32[]{:S(2)}, u32[]{:S(2)}) collective-permute-start(f32[10,16,256]{2,1,0:T(8,128)S(1)} %get-tuple-element.37), channel_id=1, source_target_pairs={{0,16},{32,48},{64,80},{96,112},{128,144},{160,176},{192,208},{224... | collective-permute-start | bytes 491528 | tf_op jit(solution)/shard_map/ppermute | solution.py:676
  11.3 7.0 %collective-permute-start.4 = (f32[10,16,128]{2,1,0:T(8,128)S(1)}, f32[10,16,128]{2,1,0:T(8,128)S(1)}, u32[]{:S(2)}, u32[]{:S(2)}) collective-permute-start(f32[10,16,128]{2,1,0:T(8,128)S(1)} %get-tuple-element.40), channel_id=1, source_target_pairs={{16,32},{48,64},{80,96},{112,128},{144,160},{176,192},{208,224},{3... | collective-permute-start | bytes 245768 | tf_op jit(solution)/shard_map/ppermute | solution.py:676
  12.0 6.4 %collective-permute-start.5 = (f32[10,16,128]{2,1,0:T(8,128)S(1)}, f32[10,16,128]{2,1,0:T(8,128)S(1)}, u32[]{:S(2)}, u32[]{:S(2)}) collective-permute-start(f32[10,16,128]{2,1,0:T(8,128)S(1)} %get-tuple-element.41), channel_id=1, source_target_pairs={{0,16},{32,48},{64,80},{96,112},{128,144},{160,176},{192,208},{224... | collective-permute-start | bytes 245768 | tf_op jit(solution)/shard_map/ppermute | solution.py:676
  18.3 6.4 %copy-start = (s32[2,16,16,256]{3,2,1,0:T(8,128)S(1)}, s32[2,16,16,256]{3,2,1,0:T(8,128)}, u32[]{:S(2)}) copy-start(s32[2,16,16,256]{3,2,1,0:T(8,128)} %param.4) | copy-start | bytes 1572868
  20.3 5.0 %collective-permute-start.6 = (f32[9,8,384]{2,1,0:T(8,128)S(1)}, f32[9,8,384]{2,1,0:T(8,128)S(1)}, u32[]{:S(2)}, u32[]{:S(2)}) collective-permute-start(f32[9,8,384]{2,1,0:T(8,128)S(1)} %get-tuple-element.48), channel_id=1, source_target_pairs={{16,32},{48,64},{80,96},{112,128},{144,160},{176,192},{208,224},{3... | collective-permute-start | bytes 331784 | tf_op jit(solution)/shard_map/ppermute | solution.py:676
  21.0 5.9 %collective-permute-start.7 = (f32[9,8,384]{2,1,0:T(8,128)S(1)}, f32[9,8,384]{2,1,0:T(8,128)S(1)}, u32[]{:S(2)}, u32[]{:S(2)}) collective-permute-start(f32[9,8,384]{2,1,0:T(8,128)S(1)} %get-tuple-element.49), channel_id=1, source_target_pairs={{0,16},{32,48},{64,80},{96,112},{128,144},{160,176},{192,208},{224... | collective-permute-start | bytes 331784 | tf_op jit(solution)/shard_map/ppermute | solution.py:676

commit v3 on v2

--- a/solution.py
+++ b/solution.py
@@ -135,8 +135,11 @@
             table[pl.ds(8 * s + c, 1), :] = jnp.full((1, 128), diff_ref[s, c], F32)
 
 
-def turn_kernel(cot, cls, table_in, own, across, inside, table):
-    table[...] = table_in[...]
+def first_kernel(out):
+    out[...] = jnp.zeros((8, 128), F32)
+
+
+def turn_kernel(cot, cls, start, own, across, inside):
     odd = lax.axis_index("gy") % 2 == 1
     left_half = iota((16, 128), 1) < HY
     for f in range(3):
@@ -181,7 +184,7 @@
     gy = lax.axis_index("gy")
     nx = 16 * lax.axis_size("gx")
     ny = 256 * lax.axis_size("gy")
-    b0, u0, b1 = keep0.at[0], keep0.at[5], keep1.at[0]
+    b0, u0, b1 = keep0[0], keep0[5], keep1[0]
 
     def look_up(values):
         cls = values.astype(jnp.int32)
@@ -206,21 +209,19 @@
 
         blocks(0, 16, size, body)
 
-    def assemble_strip(main, side, high):
+    def assemble_strip(strips, high, cut):
         second = (gx + high) % 2 == 1
 
         def plane(n):
-            return jnp.concatenate(
-                [jnp.where(second, b[n], a[n]) for a, b in (main, side)], axis=1
-            )
+            return jnp.where(second, strips[1][n], strips[0][n])
 
         lo = 20 * high
         for j in range(HX):
             for s, d in enumerate(look_up(plane(j))):
-                d0[s, lo + j] = d
+                d0[s, lo + j, :, cut] = d
         for s in range(2):
             for n in range(HX - 1):
-                b0[s, lo + 1 - high + n] = plane(HX + s * (HX - 1) + n)
+                b0[s, lo + 1 - high + n, :, cut] = plane(HX + s * (HX - 1) + n)
 
     def masks(rows, step, factor, origin):
         lane = iota((rows, LN), 1)
@@ -243,15 +244,15 @@
         def body(start):
             for s in range(2):
                 face_weights(
-                    d.at[s], keep.at[1, s], keep.at[2, s], keep.at[3, s], keep.at[4, s],
-                    keep.at[0, s], v.at[s], start, size, factor_x, my, mz, step, 0 if step == 1 else 1,
+                    d.at[s], keep[1].at[s], keep[2].at[s], keep[3].at[s], keep[4].at[s],
+                    keep[0].at[s], v.at[s], start, size, factor_x, my, mz, step, 0 if step == 1 else 1,
                 )
 
         return body
 
     def planes(keep, u, s, start, size, step):
         return stencil(
-            u.at[s], keep.at[0, s], keep.at[1, s], keep.at[2, s], keep.at[3, s],
+            u.at[s], keep[0].at[s], keep[1].at[s], keep[2].at[s], keep[3].at[s],
             start, size, step, 0 if step == 1 else 1,
         )
 
@@ -262,7 +263,7 @@
         def body(start):
             for s in range(2):
                 for p, here, r in planes(keep, v, s, start, size, step):
-                    keep[5, s, p] = here + keep[4, s, p] * r
+                    keep[5][s, p] = here + keep[4][s, p] * r
 
         return body
 
@@ -297,10 +298,17 @@
 COARSER = 0.5 * STEP
 
 
-def own_kernel(table, own, edge, keep0, keep1, d0, v0, d1):
-    assemble_own, _, weigh, smooth, restrict, coarse_diff, _ = fine_tools(
+def own_kernel(table, own, edge, mfirst, msecond, *refs):
+    keep0, keep1, (d0, v0, d1) = refs[:6], refs[6:12], refs[12:]
+    assemble_own, at, weigh, smooth, restrict, coarse_diff, _ = fine_tools(
         table, keep0, keep1, d0, v0, d1
     )
+
+    def one_side(high, carry):
+        at[0]((mfirst, msecond), high, slice(0, 256))
+        return carry
+
+    lax.fori_loop(0, 2, one_side, 0)
     assemble_own(own, edge, 4)
     weigh(5, 19, 7, 16, 1, FINE, d0, keep0, v0)
     smooth(6, 18, 4, keep0, v0, 1)
@@ -309,9 +317,10 @@
 
 
 def near_kernel(
-    table, mfirst, msecond, sfirst, ssecond, keep0_in, keep1_in, d0_in, v0_in, d1_in,
-    first, second, keep0, keep1, d0, v0, d1,
+    table, sfirst, ssecond, *refs,
 ):
+    first, second, *refs = refs[15:]
+    keep0, keep1, (d0, v0, d1) = refs[:6], refs[6:12], refs[12:]
     _, at, _, _, _, _, _ = fine_tools(table, keep0, keep1, d0, v0, d1)
     assemble_strip, weigher, smoother, restricter = at
     weigh = weigher(4, 16, 1, FINE, d0, keep0, v0)
@@ -319,7 +328,7 @@
     restrict = restricter(2)
 
     def one_side(high, carry):
-        assemble_strip((mfirst, msecond), (sfirst, ssecond), high)
+        assemble_strip((sfirst, ssecond), high, slice(256, LN))
         weigh(1 + 18 * high)
         smooth(2 + 16 * high)
         restrict(6 + 6 * high)
@@ -335,7 +344,7 @@
         second[n] = jnp.where(odd, low, high)
 
     for k in range(4):
-        send(k, keep1.at[0], 6 + k, 10 + k)
+        send(k, keep1[0], 6 + k, 10 + k)
     for k in range(5):
         send(4 + k, d1, 6 + k, 9 + k)
 
@@ -366,7 +375,8 @@
         message[k] = jnp.where(lane < 96, halved[k], pltpu.roll(halved[3], 96 - 32 * k, 1))
 
 
-def inner_kernel(keep1_in, d1, counts, keep1, v1, react, diff2, matrix, zs):
+def inner_kernel(d1, counts, *refs):
+    keep1, (v1, react, diff2, matrix, zs) = refs[6:12], refs[12:]
     _, _, weigh, smooth, _, _, _ = fine_tools(None, keep1, keep1, None, None, d1)
     weigh(7, 13, 6, 8, 2, COARSER, d1, keep1, v1)
     smooth(8, 12, 4, keep1, v1, 2)
@@ -379,11 +389,9 @@
     to_level2(rows, matrix[...], zs, diff2)
 
 
-def outer_kernel(
-    first, second, diff2, matrix, keep1_in, v1_in, d1_in,
-    message, keep1, v1, d1,
-    zs,
-):
+def outer_kernel(first, second, diff2, matrix, *refs):
+    message, *refs = refs[8:]
+    keep1, (v1, d1, zs) = refs[:6], refs[6:]
     _, _, weigh, smooth, _, _, planes = fine_tools(None, keep1, keep1, None, None, d1)
     gx = lax.axis_index("gx")
     last = lax.axis_size("gx") - 1
@@ -400,8 +408,8 @@
         low = jnp.where(odd, second[k], first[k])
         high = jnp.where(odd, first[k], second[k])
         if k < 4:
-            both(low, keep1.at[0], 2 + k)
-            both(high, keep1.at[0], 14 + k)
+            both(low, keep1[0], 2 + k)
+            both(high, keep1[0], 14 + k)
         else:
             both(low, d1, k - 3, gx > 0)
             both(high, d1, 10 + k, gx < last)
@@ -409,7 +417,7 @@
         weigh(start, start + 5, 5, 8, 2, COARSER, d1, keep1, v1)
     for start in (3, 12):
         smooth(start, start + 5, 5, keep1, v1, 2)
-    res = [[r for _, _, r in planes(keep1, keep1.at[5], s, 6, 8, 2)] for s in range(2)]
+    res = [[r for _, _, r in planes(keep1, keep1[5], s, 6, 8, 2)] for s in range(2)]
     rows = [res[s][2 * n] + res[s][2 * n + 1] for n in range(4) for s in range(2)]
     to_level2(rows, matrix[...], zs, message.at[0])
     message[1] = diff2[...]
@@ -538,10 +546,9 @@
 
 
 def up_kernel(
-    tiles, keep2, keep3, keep0, keep1, react,
-    out,
-    c4, rep2, u3, u2, c2, p1, q1, q0,
+    tiles, keep2, keep3, react, *refs,
 ):
+    keep0, keep1, (out, c4, rep2, u3, u2, c2, p1, q1, q0) = refs[:6], refs[6:12], refs[12:]
     gx = lax.axis_index("gx")
     gy = lax.axis_index("gy")
 
@@ -598,7 +605,7 @@
 
     def planes(keep, u, s, start, size, step):
         return stencil(
-            u.at[s], keep.at[0, s], keep.at[1, s], keep.at[2, s], keep.at[3, s],
+            u.at[s], keep[0].at[s], keep[1].at[s], keep[2].at[s], keep[3].at[s],
             start, size, step, 0 if step == 1 else 1,
         )
 
@@ -606,13 +613,13 @@
         def body(start):
             for s in range(2):
                 for p, here, r in planes(keep, u, s, start, size, step):
-                    new[s, p] = here + keep[4, s, p] * r
+                    new[s, p] = here + keep[4][s, p] * r
 
         blocks(lo, hi, size, body)
 
     for i in range(3, 17):
         for s in range(2):
-            p1[s, i] = keep1[5, s, i] + c2[(i - 6) // 2 + 2, s]
+            p1[s, i] = keep1[5][s, i] + c2[(i - 6) // 2 + 2, s]
     smooth(4, 16, 12, keep1, p1, q1, 2)
     smooth(5, 15, 10, keep1, q1, p1, 2)
 
@@ -621,15 +628,15 @@
         for s in range(2):
             spread = [p1[s, 5 + 3 * n + j] for j in range(4)]
             spread = [jnp.concatenate([c, c], axis=0) for c in spread]
-            u = [keep0[5, s, start - 1 + j] + spread[j // 2] for j in range(8)]
-            fx = keep0[1, s, start] * (u[1] - u[0])
+            u = [keep0[5][s, start - 1 + j] + spread[j // 2] for j in range(8)]
+            fx = keep0[1][s, start] * (u[1] - u[0])
             for j in range(6):
                 p = start + j
-                fxn = keep0[1, s, p + 1] * (u[j + 2] - u[j + 1])
+                fxn = keep0[1][s, p + 1] * (u[j + 2] - u[j + 1])
                 r = residual(
-                    u[j + 1], keep0[0, s, p], fx, fxn, keep0[2, s, p], keep0[3, s, p], 1, 0
+                    u[j + 1], keep0[0][s, p], fx, fxn, keep0[2][s, p], keep0[3][s, p], 1, 0
                 )
-                q0[s, p] = u[j + 1] + keep0[4, s, p] * r
+                q0[s, p] = u[j + 1] + keep0[4][s, p] * r
                 fx = fxn
         return carry
 
@@ -639,7 +646,7 @@
         adj = [[], []]
         for s in range(2):
             for p, here, r in planes(keep0, q0, s, start, 4, 1):
-                adj[s].append((here + keep0[4, s, p] * r)[:, :256])
+                adj[s].append((here + keep0[4][s, p] * r)[:, :256])
         for j in range(4):
             x = start + j - HX
             a0, a1 = adj[0][j], adj[1][j]
@@ -686,11 +693,12 @@
     shape = cotangent.shape
     counts, cotangent = (a.reshape(2, 8, 2, 16, 256) for a in (counts, cotangent))
     classes = classes.reshape(8, 2, 16, 256)
-    (table,) = call(table_kernel, [(16, 128)], [], (diffusivity,), "table", 8, "s", cycles=10**9)
-    own, across, inside, table = call(
+    (start,) = call(first_kernel, [(8, 128)], [], (), "first", 8, cycles=10**9)
+    (table,) = call(table_kernel, [(16, 128)], [], (diffusivity,), "table", 8, "s")
+    own, across, inside = call(
         turn_kernel,
-        [(16, 3, 16, 256), (8, 3, 16, 128), (8, 3, 16, 128), (16, 128)], [],
-        (cotangent, classes, table), "turn", 8,
+        [(16, 3, 16, 256), (8, 3, 16, 128), (8, 3, 16, 128)], [],
+        (cotangent, classes, start), "turn", 8,
     )
     across, inside = swap("gy", 1, across), swap("gy", 0, inside)
     strip = (3 * HX - 2, 16, 256)
@@ -701,28 +709,28 @@
         edge_kernel, [(16, 3, 16, 128), strip, strip], [], (across, inside), "edge", 8
     )
     sfirst, ssecond = swap("gx", 1, sfirst), swap("gx", 0, ssecond)
-    fine = [(6, 2, NPL, 16, LN), (6, 2, N1, 8, LN)]
-    fine += [(2, NPL, 16, LN)] * 2 + [(2, N1, 8, LN)]
-    kept = call(own_kernel, fine, [], (table, own, edge), "own", 8, cycles=10**7)
+    level0, level1 = (2, NPL, 16, LN), (2, N1, 8, LN)
+    fine = [level0] * 6 + [level1] * 6 + [level0] * 2 + [level1]
+    kept = call(own_kernel, fine, [], (table, own, edge, mfirst, msecond), "own", 8, cycles=10**7)
     strip = (9, 8, LN)
-    first, second, keep0, keep1, _, _, d1 = call(
+    first, second, *kept = call(
         near_kernel,
         [strip, strip] + fine, [],
-        (table, mfirst, msecond, sfirst, ssecond, *kept), "near", 8,
-        aliases={5 + n: 2 + n for n in range(5)},
-    )
+        (table, sfirst, ssecond, *kept), "near", 8,
+        aliases={3 + n: 2 + n for n in range(15)},
+    )
+    keep0, keep1, d1 = kept[:6], kept[6:12], kept[14]
     first, second = swap("gx", 1, first), swap("gx", 0, second)
-    level1 = [(6, 2, N1, 8, LN), (2, N1, 8, LN), (2, N1, 8, LN)]
     zs = (4, 16, 128)
-    keep1, v1, react, diff2, matrix = call(
-        inner_kernel, level1[:2] + [(16, 2, 16, 256), (3, 8, 128), (LN, 128)], [zs],
-        (keep1, d1, counts), "inner", 8,
-        aliases={0: 0}, cycles=10**7, dtypes=[F32] * 4 + [BF16],
-    )
-    message, keep1, _, _ = call(
-        outer_kernel, [(2, 3, 8, 128)] + level1, [zs],
-        (first, second, diff2, matrix, keep1, v1, d1), "outer", 8,
-        aliases={4: 1, 5: 2, 6: 3},
+    *keep1, v1, react, diff2, matrix = call(
+        inner_kernel, [level1] * 7 + [(16, 2, 16, 256), (3, 8, 128), (LN, 128)], [zs],
+        (d1, counts, *keep1), "inner", 8,
+        aliases={2 + n: n for n in range(6)}, cycles=10**7, dtypes=[F32] * 9 + [BF16],
+    )
+    message, *keep1, _, _ = call(
+        outer_kernel, [(2, 3, 8, 128)] + [level1] * 8, [zs],
+        (first, second, diff2, matrix, *keep1, v1, d1), "outer", 8,
+        aliases={4 + n: 1 + n for n in range(8)},
     )
     gathered = everyone(message, "gx")
     tile, keep2, keep3 = call(
@@ -739,7 +747,7 @@
             (2, X4 + 16, 128), (128, 128), (10, 8, 128), (12, 8, 128), (8, 2, 8, LN),
             (2, N1, 8, LN), (2, N1, 8, LN), (2, NPL, 16, LN),
         ],
-        (tiles, keep2, keep3, keep0, keep1, react), "up", 12,
+        (tiles, keep2, keep3, react, *keep0, *keep1), "up", 12,
     )
     return gradient.reshape(shape)
 

time: 70.9 us -> 70.5 us (level)
    pallas_call x10 -> x11, Pallas kernels: 14.2 us -> 14.1 us  [call(): pl.pallas_call(kernel, out_shape=[jax.ShapeDtypeStruct(o, d) for o, d in...]
  transfers between devices with their start and end apart: 8 -> 8, of which waited for: 1 -> 1; matrix products, arithmetic and copies ran while one was open for 0% -> 0% of each run, Pallas kernels for 5% -> 6%
where the time goes in v3:
time: 70.5 us; the launch traced here: 70.2 us
  blocking collectives  35.2 us (50%)
  starting transfers between devices  18 us (26%)
  Pallas kernels  14.1 us (20%)
  waiting for transfers between devices  1.57 us (2%)
  local copies, waits for them, and re-layouts  1.14 us (2%)
    all_to_all x2, blocking collectives, everyone(): return lax.all_to_all(copies, axis, split_axis=0, concat_axis=0, tiled=True)  35.2 us
    ppermute x8, starting transfers between devices, swap(): return lax.ppermute(block, axis, pairs + [(j, i) for i, j in pairs])  18 us
    pallas_call x11, Pallas kernels, call(): pl.pallas_call(kernel, out_shape=[jax.ShapeDtypeStruct(o, d) for o, d in...  14.1 us
    ppermute x8, waiting for transfers between devices, swap(): return lax.ppermute(block, axis, pairs + [(j, i) for i, j in pairs])  1.57 us
  transfers between devices with their start and end apart: 8, of which 1 were waited for; matrix products, arithmetic and copies ran while one was open for 0% of the time, Pallas kernels for 6%

profile of v3, /device:TPU:1, one launch (start us, length us, event | category | flops | bytes accessed | tf_op | source)
XLA Modules:
  0.0 70.2 jit_solution(2038260684554618381)
XLA Ops:
  0.0 0.0 copy-start.1
  0.0 0.0 copy-start.2
  0.0 0.0 copy-start.3
  0.0 1.0 %copy-done.1 = f32[2,16,16,256]{3,2,1,0:T(8,128)S(1)} copy-done((f32[2,16,16,256]{3,2,1,0:T(8,128)S(1)}, f32[2,16,16,256]{3,2,1,0:T(8,128)}, u32[]{:S(2)}) %copy-start.1) | copy-done | bytes 524312
  1.0 0.1 copy-done.2
  1.1 0.3 turn.1
  1.4 4.9 %collective-permute-start = (f32[8,3,16,128]{3,2,1,0:T(8,128)S(1)}, f32[8,3,16,128]{3,2,1,0:T(8,128)S(1)}, u32[]{:S(2)}, u32[]{:S(2)}) collective-permute-start(f32[8,3,16,128]{3,2,1,0:T(8,128)S(1)} %get-tuple-element.63), channel_id=1, source_target_pairs={{1,2},{3,4},{5,6},{7,8},{9,10},{11,12},{13,14},{2,1},{4,3},{6,5},{... | collective-permute-start | bytes 589832 | tf_op jit(solution)/shard_map/ppermute | solution.py:683
  6.3 0.1 collective-permute-start.1
  6.5 0.7 collective-permute-start.4
  7.2 3.7 %collective-permute-start.5 = (f32[10,16,256]{2,1,0:T(8,128)S(1)}, f32[10,16,256]{2,1,0:T(8,128)S(1)}, u32[]{:S(2)}, u32[]{:S(2)}) collective-permute-start(f32[10,16,256]{2,1,0:T(8,128)S(1)} %get-tuple-element.70), channel_id=1, source_target_pairs={{0,16},{32,48},{64,80},{96,112},{128,144},{160,176},{192,208},{224... | collective-permute-start | bytes 491528 | tf_op jit(solution)/shard_map/ppermute | solution.py:683
  10.9 0.0 collective-permute-done.across
  10.9 0.0 collective-permute-done.1.inside
  10.9 0.1 edge.1
  11.0 0.7 collective-permute-start.2
  11.7 3.5 %collective-permute-start.3 = (f32[10,16,128]{2,1,0:T(8,128)S(1)}, f32[10,16,128]{2,1,0:T(8,128)S(1)}, u32[]{:S(2)}, u32[]{:S(2)}) collective-permute-start(f32[10,16,128]{2,1,0:T(8,128)S(1)} %get-tuple-element.66), channel_id=1, source_target_pairs={{0,16},{32,48},{64,80},{96,112},{128,144},{160,176},{192,208},{224... | collective-permute-start | bytes 245768 | tf_op jit(solution)/shard_map/ppermute | solution.py:683
  15.2 0.0 copy-done.3
  15.2 0.6 table.1
  15.7 0.0 collective-permute-done.4.mfirst
  15.8 0.0 collective-permute-done.5.msecond
  15.8 3.0 %own.1 = (f32[2,24,16,384]{3,2,1,0:T(8,128)S(1)}, f32[2,24,16,384]{3,2,1,0:T(8,128)S(1)}, f32[2,24,16,384]{3,2,1,0:T(8,128)S(1)}, f32[2,24,16,384]{3,2,1,0:T(8,1...) custom-call(f32[16,128]{1,0:T(8,128)S(1)} %table.1, ...), custom_call_target="tpu_custom_call" | custom-call | flops 10000000 | tf_op jit(solution)/shard_map/own/pallas_call | solution.py:666
  18.7 0.0 collective-permute-done.2.sfirst
  18.8 0.0 collective-permute-done.3.ssecond
  18.8 0.0 copy-start
  18.8 1.8 %near.1 = (f32[9,8,384]{2,1,0:T(8,128)S(1)}, f32[9,8,384]{2,1,0:T(8,128)S(1)}, f32[2,24,16,384]{3,2,1,0:T(8,128)S(1)}, f32[2,24,16,384]{3,2,1,0:T(8,128)S(1)}, f...) custom-call(f32[16,128]{1,0:T(8,128)S(1)} %table.1, ...), custom_call_target="tpu_custom_call", output_to_operand_aliasing={{2}: (3, {}), {3}: (4, {}), {4}: (5, {}), {5}: (6, {}), {6}... | custom-call | tf_op jit(solution)/shard_map/near/pallas_call | solution.py:666
  20.6 0.7 collective-permute-start.6
  21.3 3.7 %collective-permute-start.7 = (f32[9,8,384]{2,1,0:T(8,128)S(1)}, f32[9,8,384]{2,1,0:T(8,128)S(1)}, u32[]{:S(2)}, u32[]{:S(2)}) collective-permute-start(f32[9,8,384]{2,1,0:T(8,128)S(1)} %get-tuple-element.87), channel_id=1, source_target_pairs={{0,16},{32,48},{64,80},{96,112},{128,144},{160,176},{192,208},{224... | collective-permute-start | bytes 331784 | tf_op jit(solution)/shard_map/ppermute | solution.py:683
  25.0 0.0 copy-done
  25.0 0.6 inner.1
  25.6 0.0 collective-permute-done.6.first
  25.6 1.6 %collective-permute-done.7.second = f32[9,8,384]{2,1,0:T(8,128)S(1)} collective-permute-done((f32[9,8,384]{2,1,0:T(8,128)S(1)}, f32[9,8,384]{2,1,0:T(8,128)S(1)}, u32[]{:S(2)}, u32[]{:S(2)}) %collective-permute-start.7) | collective-permute-done | bytes 110624 | tf_op jit(solution)/shard_map/ppermute | solution.py:683
  27.1 0.9 %outer.1 = (f32[2,3,8,128]{3,2,1,0:T(8,128)S(1)}, f32[2,20,8,384]{3,2,1,0:T(8,128)S(1)}, f32[2,20,8,384]{3,2,1,0:T(8,128)S(1)}, f32[2,20,8,384]{3,2,1,0:T(8,128)...) custom-call(f32[9,8,384]{2,1,0:T(8,128)S(1)} %collective-permute-don, ...), custom_call_target="tpu_custom_call", output_to_operand_aliasing={{1}: (4, {}), {2}: (5, {}), {3}: (6, {}), {4}: (7, {}), {5}... | custom-call | tf_op jit(solution)/shard_map/outer/pallas_call | solution.py:666
  28.1 15.6 %all_to_all.10.gathered = f32[16,2,3,8,128]{4,3,2,1,0:T(8,128)S(1)} all-to-all(f32[16,2,3,8,128]{4,3,2,1,0:T(8,128)S(1)} %broadcast_in_dim.4), channel_id=1, replica_groups=mesh['gx'=16,'gy'=16] {'gx'}, dimensions={0} | all-to-all | bytes 786432 | tf_op jit(solution)/shard_map/all_to_all | solution.py:689
  43.7 2.1 %middle.1 = (f32[8,128]{1,0:T(8,128)S(1)}, f32[6,72,8,128]{3,2,1,0:T(8,128)S(1)}, f32[6,40,8,128]{3,2,1,0:T(8,128)S(1)}) custom-call(f32[16,2,3,8,128]{4,3,2,1,0:T(8,128)S(1)} %all_to_all.10.gathered), custom_call_target="tpu_custom_call" | custom-call | tf_op jit(solution)/shard_map/middle/pallas_call | solution.py:666
  45.8 19.6 %all_to_all.11.tiles = f32[16,8,128]{2,1,0:T(8,128)S(1)} all-to-all(f32[16,8,128]{2,1,0:T(8,128)S(1)} %broadcast_in_dim.5), channel_id=1, replica_groups=mesh['gx'=16,'gy'=16] {'gy'}, dimensions={0} | all-to-all | bytes 131072 | tf_op jit(solution)/shard_map/all_to_all | solution.py:689
  65.5 4.8 %up.1 = f32[2,8,2,16,256]{4,3,2,1,0:T(8,128)} custom-call(f32[16,8,128]{2,1,0:T(8,128)S(1)} %all_to_all.11.tiles, f32[6,72,8,128]{3,2,1,0:T(8,128)S(1)} %get-tuple-element.106.keep2, f32[6,40,8,128]{3,2,1,0:T(8,128)S(1)} %get-tuple-element.107.keep3, f32[16,2,16,256]{3,2,1,0:T(8,128)S(1)} %get-tuple-element.108.react, ...), custom_call_target="tpu_custom_call" | custom-call | tf_op jit(solution)/shard_map/up/pallas_call | solution.py:666
  (4 shorter events, 0.1 us)
Async XLA Ops:
  0.0 1.0 %copy-start.1 = (f32[2,16,16,256]{3,2,1,0:T(8,128)S(1)}, f32[2,16,16,256]{3,2,1,0:T(8,128)}, u32[]{:S(2)}) copy-start(f32[2,16,16,256]{3,2,1,0:T(8,128)} %param.7) | copy-start | bytes 1572868
  0.0 1.1 %copy-start.2 = (s32[16,16,256]{2,1,0:T(8,128)S(1)}, s32[16,16,256]{2,1,0:T(8,128)}, u32[]{:S(2)}) copy-start(s32[16,16,256]{2,1,0:T(8,128)} %param.5) | copy-start | bytes 786436
  0.0 15.2 %copy-start.3 = (f32[2,8]{1,0:T(2,128)S(1)}, f32[2,8]{1,0:T(2,128)}, u32[]{:S(2)}) copy-start(f32[2,8]{1,0:T(2,128)} %diff_ref.1) | copy-start | bytes 196
  1.4 9.5 %collective-permute-start = (f32[8,3,16,128]{3,2,1,0:T(8,128)S(1)}, f32[8,3,16,128]{3,2,1,0:T(8,128)S(1)}, u32[]{:S(2)}, u32[]{:S(2)}) collective-permute-start(f32[8,3,16,128]{3,2,1,0:T(8,128)S(1)} %get-tuple-element.63), channel_id=1, source_target_pairs={{1,2},{3,4},{5,6},{7,8},{9,10},{11,12},{13,14},{2,1},{4,3},{6,5},{... | collective-permute-start | bytes 589832 | tf_op jit(solution)/shard_map/ppermute | solution.py:683
  6.3 4.6 %collective-permute-start.1 = (f32[8,3,16,128]{3,2,1,0:T(8,128)S(1)}, f32[8,3,16,128]{3,2,1,0:T(8,128)S(1)}, u32[]{:S(2)}, u32[]{:S(2)}) collective-permute-start(f32[8,3,16,128]{3,2,1,0:T(8,128)S(1)} %get-tuple-element.64), channel_id=1, source_target_pairs={{0,1},{2,3},{4,5},{6,7},{8,9},{10,11},{12,13},{14,15},{1,0},{3,2},... | collective-permute-start | bytes 589832 | tf_op jit(solution)/shard_map/ppermute | solution.py:683
  6.5 9.3 %collective-permute-start.4 = (f32[10,16,256]{2,1,0:T(8,128)S(1)}, f32[10,16,256]{2,1,0:T(8,128)S(1)}, u32[]{:S(2)}, u32[]{:S(2)}) collective-permute-start(f32[10,16,256]{2,1,0:T(8,128)S(1)} %get-tuple-element.69), channel_id=1, source_target_pairs={{16,32},{48,64},{80,96},{112,128},{144,160},{176,192},{208,224},{3... | collective-permute-start | bytes 491528 | tf_op jit(solution)/shard_map/ppermute | solution.py:683
  7.2 8.6 %collective-permute-start.5 = (f32[10,16,256]{2,1,0:T(8,128)S(1)}, f32[10,16,256]{2,1,0:T(8,128)S(1)}, u32[]{:S(2)}, u32[]{:S(2)}) collective-permute-start(f32[10,16,256]{2,1,0:T(8,128)S(1)} %get-tuple-element.70), channel_id=1, source_target_pairs={{0,16},{32,48},{64,80},{96,112},{128,144},{160,176},{192,208},{224... | collective-permute-start | bytes 491528 | tf_op jit(solution)/shard_map/ppermute | solution.py:683
  11.0 7.7 %collective-permute-start.2 = (f32[10,16,128]{2,1,0:T(8,128)S(1)}, f32[10,16,128]{2,1,0:T(8,128)S(1)}, u32[]{:S(2)}, u32[]{:S(2)}) collective-permute-start(f32[10,16,128]{2,1,0:T(8,128)S(1)} %get-tuple-element.65), channel_id=1, source_target_pairs={{16,32},{48,64},{80,96},{112,128},{144,160},{176,192},{208,224},{3... | collective-permute-start | bytes 245768 | tf_op jit(solution)/shard_map/ppermute | solution.py:683
  11.7 7.0 %collective-permute-start.3 = (f32[10,16,128]{2,1,0:T(8,128)S(1)}, f32[10,16,128]{2,1,0:T(8,128)S(1)}, u32[]{:S(2)}, u32[]{:S(2)}) collective-permute-start(f32[10,16,128]{2,1,0:T(8,128)S(1)} %get-tuple-element.66), channel_id=1, source_target_pairs={{0,16},{32,48},{64,80},{96,112},{128,144},{160,176},{192,208},{224... | collective-permute-start | bytes 245768 | tf_op jit(solution)/shard_map/ppermute | solution.py:683
  18.8 6.2 %copy-start = (s32[2,16,16,256]{3,2,1,0:T(8,128)S(1)}, s32[2,16,16,256]{3,2,1,0:T(8,128)}, u32[]{:S(2)}) copy-start(s32[2,16,16,256]{3,2,1,0:T(8,128)} %param.4) | copy-start | bytes 1572868
  20.6 5.0 %collective-permute-start.6 = (f32[9,8,384]{2,1,0:T(8,128)S(1)}, f32[9,8,384]{2,1,0:T(8,128)S(1)}, u32[]{:S(2)}, u32[]{:S(2)}) collective-permute-start(f32[9,8,384]{2,1,0:T(8,128)S(1)} %get-tuple-element.86), channel_id=1, source_target_pairs={{16,32},{48,64},{80,96},{112,128},{144,160},{176,192},{208,224},{3... | collective-permute-start | bytes 331784 | tf_op jit(solution)/shard_map/ppermute | solution.py:683
  21.3 5.9 %collective-permute-start.7 = (f32[9,8,384]{2,1,0:T(8,128)S(1)}, f32[9,8,384]{2,1,0:T(8,128)S(1)}, u32[]{:S(2)}, u32[]{:S(2)}) collective-permute-start(f32[9,8,384]{2,1,0:T(8,128)S(1)} %get-tuple-element.87), channel_id=1, source_target_pairs={{0,16},{32,48},{64,80},{96,112},{128,144},{160,176},{192,208},{224... | collective-permute-start | bytes 331784 | tf_op jit(solution)/shard_map/ppermute | solution.py:683

commit v4 on v3

--- a/solution.py
+++ b/solution.py
@@ -132,7 +132,8 @@
 def table_kernel(diff_ref, table):
     for s in range(2):
         for c in range(8):
-            table[pl.ds(8 * s + c, 1), :] = jnp.full((1, 128), diff_ref[s, c], F32)
+            value = diff_ref[pl.ds(s, 1), pl.ds(c, 1)]
+            table[pl.ds(8 * s + c, 1), :] = jnp.broadcast_to(value, (1, 128))
 
 
 def first_kernel(out):
@@ -474,18 +475,18 @@
             fourth = jnp.where(lane < 32, fourth[0], jnp.where(lane < 64, fourth[1], fourth[2]))
             for k, plane in enumerate(packed + [fourth]):
                 ref[PAD + 4 * g + k] = plane
-    planes2 = level(keep2, d2, v2, X2, 32, 1, 1, 0.0625, ny // 4)
+    planes2 = level(keep2, d2, v2, X2, X2, 1, 1, 0.0625, ny // 4)
 
     def restrict(start):
         first = 2 * (start - PAD) + PAD
-        res = [r for _, _, r in planes2(keep2.at[5], first, 32)]
-        for i in range(16):
+        res = [r for _, _, r in planes2(keep2.at[5], first, X2)]
+        for i in range(X3):
             total = res[2 * i] + res[2 * i + 1]
             keep3[0, start + i] = 0.125 * pair_rows(pair_lanes(total, 1), 1)
             total = d2[first + 2 * i] + d2[first + 2 * i + 1]
             d3[start + i] = 0.125 * pair_rows(pair_lanes(total, 1), 1)
 
-    blocks(PAD, PAD + X3, 16, restrict)
+    blocks(PAD, PAD + X3, X3, restrict)
     planes3 = level(keep3, d3, v3, X3, 32, 2, 2, 0.015625, ny // 4)
 
     def gather_pair(total):
@@ -548,7 +549,7 @@
 def up_kernel(
     tiles, keep2, keep3, react, *refs,
 ):
-    keep0, keep1, (out, c4, rep2, u3, u2, c2, p1, q1, q0) = refs[:6], refs[6:12], refs[12:]
+    keep0, keep1, (out, c4, rep2, u3, u2, p1, q1, q0) = refs[:6], refs[6:12], refs[12:]
     gx = lax.axis_index("gx")
     gy = lax.axis_index("gy")
 
@@ -600,8 +601,7 @@
     quarter = iota((1, 128), 1) // 4
     edge = jnp.where(quarter < 16, quarter + 80, quarter - 16)
     flat = [pick_lanes(rep2[...], lanes) for lanes in (quarter + 16, quarter + 48, edge)]
-    flat = jnp.concatenate(flat, axis=1)
-    c2[...] = flat.reshape(8, 2, 8, LN)
+    c2 = jnp.concatenate(flat, axis=1).reshape(8, 2, 8, LN)
 
     def planes(keep, u, s, start, size, step):
         return stencil(
@@ -694,7 +694,7 @@
     counts, cotangent = (a.reshape(2, 8, 2, 16, 256) for a in (counts, cotangent))
     classes = classes.reshape(8, 2, 16, 256)
     (start,) = call(first_kernel, [(8, 128)], [], (), "first", 8, cycles=10**9)
-    (table,) = call(table_kernel, [(16, 128)], [], (diffusivity,), "table", 8, "s")
+    (table,) = call(table_kernel, [(16, 128)], [], (diffusivity,), "table", 8)
     own, across, inside = call(
         turn_kernel,
         [(16, 3, 16, 256), (8, 3, 16, 128), (8, 3, 16, 128)], [],
@@ -744,7 +744,7 @@
         up_kernel,
         [(2, 8, 2, 16, 256)],
         [
-            (2, X4 + 16, 128), (128, 128), (10, 8, 128), (12, 8, 128), (8, 2, 8, LN),
+            (2, X4 + 16, 128), (128, 128), (10, 8, 128), (12, 8, 128),
             (2, N1, 8, LN), (2, N1, 8, LN), (2, NPL, 16, LN),
         ],
         (tiles, keep2, keep3, react, *keep0, *keep1), "up", 12,

time: 70.5 us -> 69.9 us (level)
  Pallas kernels: 14.1 us -> 13.1 us
    pallas_call x11, Pallas kernels: 14.1 us -> 13.1 us  [call(): pl.pallas_call(kernel, out_shape=[jax.ShapeDtypeStruct(o, d) for o, d in...]
  transfers between devices with their start and end apart: 8 -> 8, of which waited for: 1 -> 1; matrix products, arithmetic and copies ran while one was open for 0% -> 0% of each run, Pallas kernels for 6% -> 5%
where the time goes in v4:
time: 69.9 us; the launch traced here: 69.7 us
  blocking collectives  35.7 us (51%)
  starting transfers between devices  18 us (26%)
  Pallas kernels  13.1 us (19%)
  waiting for transfers between devices  1.57 us (2%)
  local copies, waits for them, and re-layouts  1.14 us (2%)
    all_to_all x2, blocking collectives, everyone(): return lax.all_to_all(copies, axis, split_axis=0, concat_axis=0, tiled=True)  35.7 us
    ppermute x8, starting transfers between devices, swap(): return lax.ppermute(block, axis, pairs + [(j, i) for i, j in pairs])  18 us
    pallas_call x11, Pallas kernels, call(): pl.pallas_call(kernel, out_shape=[jax.ShapeDtypeStruct(o, d) for o, d in...  13.1 us
    ppermute x8, waiting for transfers between devices, swap(): return lax.ppermute(block, axis, pairs + [(j, i) for i, j in pairs])  1.57 us
  transfers between devices with their start and end apart: 8, of which 1 were waited for; matrix products, arithmetic and copies ran while one was open for 0% of the time, Pallas kernels for 5%

profile of v4, /device:TPU:1, one launch (start us, length us, event | category | flops | bytes accessed | tf_op | source)
XLA Modules:
  0.0 69.7 jit_solution(1745735216592151542)
XLA Ops:
  0.0 0.0 copy-start.1
  0.0 0.0 copy-start.2
  0.0 0.0 copy-start.3
  0.0 1.0 %copy-done.1 = f32[2,16,16,256]{3,2,1,0:T(8,128)S(1)} copy-done((f32[2,16,16,256]{3,2,1,0:T(8,128)S(1)}, f32[2,16,16,256]{3,2,1,0:T(8,128)}, u32[]{:S(2)}) %copy-start.1) | copy-done | bytes 524312
  1.0 0.1 copy-done.2
  1.1 0.3 turn.1
  1.4 4.9 %collective-permute-start = (f32[8,3,16,128]{3,2,1,0:T(8,128)S(1)}, f32[8,3,16,128]{3,2,1,0:T(8,128)S(1)}, u32[]{:S(2)}, u32[]{:S(2)}) collective-permute-start(f32[8,3,16,128]{3,2,1,0:T(8,128)S(1)} %get-tuple-element.63), channel_id=1, source_target_pairs={{1,2},{3,4},{5,6},{7,8},{9,10},{11,12},{13,14},{2,1},{4,3},{6,5},{... | collective-permute-start | bytes 589832 | tf_op jit(solution)/shard_map/ppermute | solution.py:683
  6.3 0.1 collective-permute-start.1
  6.5 0.7 collective-permute-start.4
  7.2 3.7 %collective-permute-start.5 = (f32[10,16,256]{2,1,0:T(8,128)S(1)}, f32[10,16,256]{2,1,0:T(8,128)S(1)}, u32[]{:S(2)}, u32[]{:S(2)}) collective-permute-start(f32[10,16,256]{2,1,0:T(8,128)S(1)} %get-tuple-element.70), channel_id=1, source_target_pairs={{0,16},{32,48},{64,80},{96,112},{128,144},{160,176},{192,208},{224... | collective-permute-start | bytes 491528 | tf_op jit(solution)/shard_map/ppermute | solution.py:683
  10.9 0.0 collective-permute-done.across
  10.9 0.0 collective-permute-done.1.inside
  10.9 0.1 edge.1
  11.0 0.7 collective-permute-start.2
  11.7 3.5 %collective-permute-start.3 = (f32[10,16,128]{2,1,0:T(8,128)S(1)}, f32[10,16,128]{2,1,0:T(8,128)S(1)}, u32[]{:S(2)}, u32[]{:S(2)}) collective-permute-start(f32[10,16,128]{2,1,0:T(8,128)S(1)} %get-tuple-element.66), channel_id=1, source_target_pairs={{0,16},{32,48},{64,80},{96,112},{128,144},{160,176},{192,208},{224... | collective-permute-start | bytes 245768 | tf_op jit(solution)/shard_map/ppermute | solution.py:683
  15.2 0.0 copy-done.3
  15.2 0.1 table.1
  15.3 0.0 collective-permute-done.4.mfirst
  15.3 0.0 collective-permute-done.5.msecond
  15.3 3.0 %own.1 = (f32[2,24,16,384]{3,2,1,0:T(8,128)S(1)}, f32[2,24,16,384]{3,2,1,0:T(8,128)S(1)}, f32[2,24,16,384]{3,2,1,0:T(8,128)S(1)}, f32[2,24,16,384]{3,2,1,0:T(8,1...) custom-call(f32[16,128]{1,0:T(8,128)S(1)} %table.1, ...), custom_call_target="tpu_custom_call" | custom-call | flops 10000000 | tf_op jit(solution)/shard_map/own/pallas_call | solution.py:666
  18.3 0.0 collective-permute-done.2.sfirst
  18.3 0.0 collective-permute-done.3.ssecond
  18.3 0.0 copy-start
  18.3 1.8 %near.1 = (f32[9,8,384]{2,1,0:T(8,128)S(1)}, f32[9,8,384]{2,1,0:T(8,128)S(1)}, f32[2,24,16,384]{3,2,1,0:T(8,128)S(1)}, f32[2,24,16,384]{3,2,1,0:T(8,128)S(1)}, f...) custom-call(f32[16,128]{1,0:T(8,128)S(1)} %table.1, ...), custom_call_target="tpu_custom_call", output_to_operand_aliasing={{2}: (3, {}), {3}: (4, {}), {4}: (5, {}), {5}: (6, {}), {6}... | custom-call | tf_op jit(solution)/shard_map/near/pallas_call | solution.py:666
  20.1 0.7 collective-permute-start.6
  20.8 3.7 %collective-permute-start.7 = (f32[9,8,384]{2,1,0:T(8,128)S(1)}, f32[9,8,384]{2,1,0:T(8,128)S(1)}, u32[]{:S(2)}, u32[]{:S(2)}) collective-permute-start(f32[9,8,384]{2,1,0:T(8,128)S(1)} %get-tuple-element.87), channel_id=1, source_target_pairs={{0,16},{32,48},{64,80},{96,112},{128,144},{160,176},{192,208},{224... | collective-permute-start | bytes 331784 | tf_op jit(solution)/shard_map/ppermute | solution.py:683
  24.5 0.0 copy-done
  24.5 0.6 inner.1
  25.1 0.0 collective-permute-done.6.first
  25.1 1.6 %collective-permute-done.7.second = f32[9,8,384]{2,1,0:T(8,128)S(1)} collective-permute-done((f32[9,8,384]{2,1,0:T(8,128)S(1)}, f32[9,8,384]{2,1,0:T(8,128)S(1)}, u32[]{:S(2)}, u32[]{:S(2)}) %collective-permute-start.7) | collective-permute-done | bytes 110624 | tf_op jit(solution)/shard_map/ppermute | solution.py:683
  26.7 0.9 %outer.1 = (f32[2,3,8,128]{3,2,1,0:T(8,128)S(1)}, f32[2,20,8,384]{3,2,1,0:T(8,128)S(1)}, f32[2,20,8,384]{3,2,1,0:T(8,128)S(1)}, f32[2,20,8,384]{3,2,1,0:T(8,128)...) custom-call(f32[9,8,384]{2,1,0:T(8,128)S(1)} %collective-permute-don, ...), custom_call_target="tpu_custom_call", output_to_operand_aliasing={{1}: (4, {}), {2}: (5, {}), {3}: (6, {}), {4}: (7, {}), {5}... | custom-call | tf_op jit(solution)/shard_map/outer/pallas_call | solution.py:666
  27.6 16.1 %all_to_all.10.gathered = f32[16,2,3,8,128]{4,3,2,1,0:T(8,128)S(1)} all-to-all(f32[16,2,3,8,128]{4,3,2,1,0:T(8,128)S(1)} %broadcast_in_dim.4), channel_id=1, replica_groups=mesh['gx'=16,'gy'=16] {'gx'}, dimensions={0} | all-to-all | bytes 786432 | tf_op jit(solution)/shard_map/all_to_all | solution.py:689
  43.7 1.5 %middle.1 = (f32[8,128]{1,0:T(8,128)S(1)}, f32[6,72,8,128]{3,2,1,0:T(8,128)S(1)}, f32[6,40,8,128]{3,2,1,0:T(8,128)S(1)}) custom-call(f32[16,2,3,8,128]{4,3,2,1,0:T(8,128)S(1)} %all_to_all.10.gathered), custom_call_target="tpu_custom_call" | custom-call | tf_op jit(solution)/shard_map/middle/pallas_call | solution.py:666
  45.3 19.6 %all_to_all.11.tiles = f32[16,8,128]{2,1,0:T(8,128)S(1)} all-to-all(f32[16,8,128]{2,1,0:T(8,128)S(1)} %broadcast_in_dim.5), channel_id=1, replica_groups=mesh['gx'=16,'gy'=16] {'gy'}, dimensions={0} | all-to-all | bytes 131072 | tf_op jit(solution)/shard_map/all_to_all | solution.py:689
  64.9 4.8 %up.1 = f32[2,8,2,16,256]{4,3,2,1,0:T(8,128)} custom-call(f32[16,8,128]{2,1,0:T(8,128)S(1)} %all_to_all.11.tiles, f32[6,72,8,128]{3,2,1,0:T(8,128)S(1)} %get-tuple-element.106.keep2, f32[6,40,8,128]{3,2,1,0:T(8,128)S(1)} %get-tuple-element.107.keep3, f32[16,2,16,256]{3,2,1,0:T(8,128)S(1)} %get-tuple-element.108.react, ...), custom_call_target="tpu_custom_call" | custom-call | tf_op jit(solution)/shard_map/up/pallas_call | solution.py:666
  (4 shorter events, 0.1 us)
Async XLA Ops:
  0.0 1.0 %copy-start.1 = (f32[2,16,16,256]{3,2,1,0:T(8,128)S(1)}, f32[2,16,16,256]{3,2,1,0:T(8,128)}, u32[]{:S(2)}) copy-start(f32[2,16,16,256]{3,2,1,0:T(8,128)} %param.7) | copy-start | bytes 1572868
  0.0 1.1 %copy-start.2 = (s32[16,16,256]{2,1,0:T(8,128)S(1)}, s32[16,16,256]{2,1,0:T(8,128)}, u32[]{:S(2)}) copy-start(s32[16,16,256]{2,1,0:T(8,128)} %param.5) | copy-start | bytes 786436
  0.0 15.2 %copy-start.3 = (f32[2,8]{1,0:T(2,128)S(1)}, f32[2,8]{1,0:T(2,128)}, u32[]{:S(2)}) copy-start(f32[2,8]{1,0:T(2,128)} %diff_ref.1) | copy-start | bytes 196
  1.4 9.5 %collective-permute-start = (f32[8,3,16,128]{3,2,1,0:T(8,128)S(1)}, f32[8,3,16,128]{3,2,1,0:T(8,128)S(1)}, u32[]{:S(2)}, u32[]{:S(2)}) collective-permute-start(f32[8,3,16,128]{3,2,1,0:T(8,128)S(1)} %get-tuple-element.63), channel_id=1, source_target_pairs={{1,2},{3,4},{5,6},{7,8},{9,10},{11,12},{13,14},{2,1},{4,3},{6,5},{... | collective-permute-start | bytes 589832 | tf_op jit(solution)/shard_map/ppermute | solution.py:683
  6.3 4.6 %collective-permute-start.1 = (f32[8,3,16,128]{3,2,1,0:T(8,128)S(1)}, f32[8,3,16,128]{3,2,1,0:T(8,128)S(1)}, u32[]{:S(2)}, u32[]{:S(2)}) collective-permute-start(f32[8,3,16,128]{3,2,1,0:T(8,128)S(1)} %get-tuple-element.64), channel_id=1, source_target_pairs={{0,1},{2,3},{4,5},{6,7},{8,9},{10,11},{12,13},{14,15},{1,0},{3,2},... | collective-permute-start | bytes 589832 | tf_op jit(solution)/shard_map/ppermute | solution.py:683
  6.5 8.8 %collective-permute-start.4 = (f32[10,16,256]{2,1,0:T(8,128)S(1)}, f32[10,16,256]{2,1,0:T(8,128)S(1)}, u32[]{:S(2)}, u32[]{:S(2)}) collective-permute-start(f32[10,16,256]{2,1,0:T(8,128)S(1)} %get-tuple-element.69), channel_id=1, source_target_pairs={{16,32},{48,64},{80,96},{112,128},{144,160},{176,192},{208,224},{3... | collective-permute-start | bytes 491528 | tf_op jit(solution)/shard_map/ppermute | solution.py:683
  7.2 8.1 %collective-permute-start.5 = (f32[10,16,256]{2,1,0:T(8,128)S(1)}, f32[10,16,256]{2,1,0:T(8,128)S(1)}, u32[]{:S(2)}, u32[]{:S(2)}) collective-permute-start(f32[10,16,256]{2,1,0:T(8,128)S(1)} %get-tuple-element.70), channel_id=1, source_target_pairs={{0,16},{32,48},{64,80},{96,112},{128,144},{160,176},{192,208},{224... | collective-permute-start | bytes 491528 | tf_op jit(solution)/shard_map/ppermute | solution.py:683
  11.0 7.2 %collective-permute-start.2 = (f32[10,16,128]{2,1,0:T(8,128)S(1)}, f32[10,16,128]{2,1,0:T(8,128)S(1)}, u32[]{:S(2)}, u32[]{:S(2)}) collective-permute-start(f32[10,16,128]{2,1,0:T(8,128)S(1)} %get-tuple-element.65), channel_id=1, source_target_pairs={{16,32},{48,64},{80,96},{112,128},{144,160},{176,192},{208,224},{3... | collective-permute-start | bytes 245768 | tf_op jit(solution)/shard_map/ppermute | solution.py:683
  11.7 6.6 %collective-permute-start.3 = (f32[10,16,128]{2,1,0:T(8,128)S(1)}, f32[10,16,128]{2,1,0:T(8,128)S(1)}, u32[]{:S(2)}, u32[]{:S(2)}) collective-permute-start(f32[10,16,128]{2,1,0:T(8,128)S(1)} %get-tuple-element.66), channel_id=1, source_target_pairs={{0,16},{32,48},{64,80},{96,112},{128,144},{160,176},{192,208},{224... | collective-permute-start | bytes 245768 | tf_op jit(solution)/shard_map/ppermute | solution.py:683
  18.3 6.2 %copy-start = (s32[2,16,16,256]{3,2,1,0:T(8,128)S(1)}, s32[2,16,16,256]{3,2,1,0:T(8,128)}, u32[]{:S(2)}) copy-start(s32[2,16,16,256]{3,2,1,0:T(8,128)} %param.4) | copy-start | bytes 1572868
  20.1 5.0 %collective-permute-start.6 = (f32[9,8,384]{2,1,0:T(8,128)S(1)}, f32[9,8,384]{2,1,0:T(8,128)S(1)}, u32[]{:S(2)}, u32[]{:S(2)}) collective-permute-start(f32[9,8,384]{2,1,0:T(8,128)S(1)} %get-tuple-element.86), channel_id=1, source_target_pairs={{16,32},{48,64},{80,96},{112,128},{144,160},{176,192},{208,224},{3... | collective-permute-start | bytes 331784 | tf_op jit(solution)/shard_map/ppermute | solution.py:683
  20.8 5.9 %collective-permute-start.7 = (f32[9,8,384]{2,1,0:T(8,128)S(1)}, f32[9,8,384]{2,1,0:T(8,128)S(1)}, u32[]{:S(2)}, u32[]{:S(2)}) collective-permute-start(f32[9,8,384]{2,1,0:T(8,128)S(1)} %get-tuple-element.87), channel_id=1, source_target_pairs={{0,16},{32,48},{64,80},{96,112},{128,144},{160,176},{192,208},{224... | collective-permute-start | bytes 331784 | tf_op jit(solution)/shard_map/ppermute | solution.py:683

commit v5 on v4

--- a/solution.py
+++ b/solution.py
@@ -98,6 +98,17 @@
         fxn = wx[p + 1] * (after - here)
         yield p, here, residual(here, b[p], fx, fxn, wy[p], wz[p], sy, sz)
         here, fx = after, fxn
+
+
+def pair_sums(residuals):
+    sums, first = [], None
+    for _, _, r in residuals:
+        if first is None:
+            first = r
+        else:
+            sums.append(first + r)
+            first = None
+    return sums
 
 
 def face_weights(d, wx, wy, wz, inv, b, u, start, count, factor_x, my, mz, sy, sz):
@@ -418,8 +429,8 @@
         weigh(start, start + 5, 5, 8, 2, COARSER, d1, keep1, v1)
     for start in (3, 12):
         smooth(start, start + 5, 5, keep1, v1, 2)
-    res = [[r for _, _, r in planes(keep1, keep1[5], s, 6, 8, 2)] for s in range(2)]
-    rows = [res[s][2 * n] + res[s][2 * n + 1] for n in range(4) for s in range(2)]
+    res = [pair_sums(planes(keep1, keep1[5], s, 6, 8, 2)) for s in range(2)]
+    rows = [res[s][n] for n in range(4) for s in range(2)]
     to_level2(rows, matrix[...], zs, message.at[0])
     message[1] = diff2[...]
 
@@ -479,9 +490,9 @@
 
     def restrict(start):
         first = 2 * (start - PAD) + PAD
-        res = [r for _, _, r in planes2(keep2.at[5], first, X2)]
+        res = pair_sums(planes2(keep2.at[5], first, X2))
         for i in range(X3):
-            total = res[2 * i] + res[2 * i + 1]
+            total = res[i]
             keep3[0, start + i] = 0.125 * pair_rows(pair_lanes(total, 1), 1)
             total = d2[first + 2 * i] + d2[first + 2 * i + 1]
             d3[start + i] = 0.125 * pair_rows(pair_lanes(total, 1), 1)
@@ -493,9 +504,9 @@
         total = total + shift_down(total, 2, 1)
         return total + shift_down(total, 2, 0)
 
-    res = [r for _, _, r in planes3(keep3.at[5], PAD, X3)]
+    res = pair_sums(planes3(keep3.at[5], PAD, X3))
     for i in range(X4):
-        coarse[0, pl.ds(8 * i, 8), :] = gather_pair(res[2 * i] + res[2 * i + 1])
+        coarse[0, pl.ds(8 * i, 8), :] = gather_pair(res[i])
         coarse[1, pl.ds(8 * i, 8), :] = gather_pair(d3[PAD + 2 * i] + d3[PAD + 2 * i + 1])
     total = jnp.zeros((8, 128), F32)
     for g in range(8):
@@ -628,34 +639,37 @@
         for s in range(2):
             spread = [p1[s, 5 + 3 * n + j] for j in range(4)]
             spread = [jnp.concatenate([c, c], axis=0) for c in spread]
-            u = [keep0[5][s, start - 1 + j] + spread[j // 2] for j in range(8)]
-            fx = keep0[1][s, start] * (u[1] - u[0])
+
+            def corrected(j):
+                return keep0[5][s, start - 1 + j] + spread[j // 2]
+
+            here = corrected(1)
+            fx = keep0[1][s, start] * (here - corrected(0))
             for j in range(6):
                 p = start + j
-                fxn = keep0[1][s, p + 1] * (u[j + 2] - u[j + 1])
-                r = residual(
-                    u[j + 1], keep0[0][s, p], fx, fxn, keep0[2][s, p], keep0[3][s, p], 1, 0
-                )
-                q0[s, p] = u[j + 1] + keep0[4][s, p] * r
+                after = corrected(j + 2)
+                fxn = keep0[1][s, p + 1] * (after - here)
+                r = residual(here, keep0[0][s, p], fx, fxn, keep0[2][s, p], keep0[3][s, p], 1, 0)
+                q0[s, p] = here + keep0[4][s, p] * r
+                here = after
                 fx = fxn
         return carry
 
     lax.fori_loop(0, 3, corrected_sweep, 0)
 
     def last(start):
-        adj = [[], []]
-        for s in range(2):
-            for p, here, r in planes(keep0, q0, s, start, 4, 1):
-                adj[s].append((here + keep0[4][s, p] * r)[:, :256])
-        for j in range(4):
-            x = start + j - HX
-            a0, a1 = adj[0][j], adj[1][j]
+        for pair in zip(*(planes(keep0, q0, s, start, 8, 1) for s in range(2))):
+            p = pair[0][0]
+            a0, a1 = (
+                (here + keep0[4][s, p] * r)[:, :256] for s, (_, here, r) in enumerate(pair)
+            )
+            x = p - HX
             total = a0 + a1
             for s, value in enumerate((a0 - react[x, 1] * total, a1 - react[x, 0] * total)):
                 out[s, :, 0, x, :] = value[:8]
                 out[s, :, 1, x, :] = value[8:]
 
-    blocks(4, 20, 4, last)
+    blocks(4, 20, 8, last)
 
 
 def call(

time: 69.9 us -> 70.2 us (level)
  no operation moved by 1% of the time
where the time goes in v5:
time: 70.2 us; the launch traced here: 69.9 us
  blocking collectives  35.7 us (51%)
  starting transfers between devices  18 us (26%)
  Pallas kernels  13.3 us (19%)
  waiting for transfers between devices  1.57 us (2%)
  local copies, waits for them, and re-layouts  1.14 us (2%)
    all_to_all x2, blocking collectives, everyone(): return lax.all_to_all(copies, axis, split_axis=0, concat_axis=0, tiled=True)  35.7 us
    ppermute x8, starting transfers between devices, swap(): return lax.ppermute(block, axis, pairs + [(j, i) for i, j in pairs])  18 us
    pallas_call x11, Pallas kernels, call(): pl.pallas_call(kernel, out_shape=[jax.ShapeDtypeStruct(o, d) for o, d in...  13.3 us
    ppermute x8, waiting for transfers between devices, swap(): return lax.ppermute(block, axis, pairs + [(j, i) for i, j in pairs])  1.57 us
  transfers between devices with their start and end apart: 8, of which 1 were waited for; matrix products, arithmetic and copies ran while one was open for 0% of the time, Pallas kernels for 5%

profile of v5, /device:TPU:1, one launch (start us, length us, event | category | flops | bytes accessed | tf_op | source)
XLA Modules:
  0.0 69.9 jit_solution(14503243024044165808)
XLA Ops:
  0.0 0.0 copy-start.1
  0.0 0.0 copy-start.2
  0.0 0.0 copy-start.3
  0.0 1.0 %copy-done.1 = f32[2,16,16,256]{3,2,1,0:T(8,128)S(1)} copy-done((f32[2,16,16,256]{3,2,1,0:T(8,128)S(1)}, f32[2,16,16,256]{3,2,1,0:T(8,128)}, u32[]{:S(2)}) %copy-start.1) | copy-done | bytes 524312
  1.0 0.1 copy-done.2
  1.1 0.3 turn.1
  1.4 4.9 %collective-permute-start = (f32[8,3,16,128]{3,2,1,0:T(8,128)S(1)}, f32[8,3,16,128]{3,2,1,0:T(8,128)S(1)}, u32[]{:S(2)}, u32[]{:S(2)}) collective-permute-start(f32[8,3,16,128]{3,2,1,0:T(8,128)S(1)} %get-tuple-element.63), channel_id=1, source_target_pairs={{1,2},{3,4},{5,6},{7,8},{9,10},{11,12},{13,14},{2,1},{4,3},{6,5},{... | collective-permute-start | bytes 589832 | tf_op jit(solution)/shard_map/ppermute | solution.py:697
  6.3 0.1 collective-permute-start.1
  6.5 0.7 collective-permute-start.4
  7.2 3.7 %collective-permute-start.5 = (f32[10,16,256]{2,1,0:T(8,128)S(1)}, f32[10,16,256]{2,1,0:T(8,128)S(1)}, u32[]{:S(2)}, u32[]{:S(2)}) collective-permute-start(f32[10,16,256]{2,1,0:T(8,128)S(1)} %get-tuple-element.70), channel_id=1, source_target_pairs={{0,16},{32,48},{64,80},{96,112},{128,144},{160,176},{192,208},{224... | collective-permute-start | bytes 491528 | tf_op jit(solution)/shard_map/ppermute | solution.py:697
  10.9 0.0 collective-permute-done.across
  10.9 0.0 collective-permute-done.1.inside
  10.9 0.1 edge.1
  11.0 0.7 collective-permute-start.2
  11.7 3.5 %collective-permute-start.3 = (f32[10,16,128]{2,1,0:T(8,128)S(1)}, f32[10,16,128]{2,1,0:T(8,128)S(1)}, u32[]{:S(2)}, u32[]{:S(2)}) collective-permute-start(f32[10,16,128]{2,1,0:T(8,128)S(1)} %get-tuple-element.66), channel_id=1, source_target_pairs={{0,16},{32,48},{64,80},{96,112},{128,144},{160,176},{192,208},{224... | collective-permute-start | bytes 245768 | tf_op jit(solution)/shard_map/ppermute | solution.py:697
  15.2 0.0 copy-done.3
  15.2 0.1 table.1
  15.3 0.0 collective-permute-done.4.mfirst
  15.3 0.0 collective-permute-done.5.msecond
  15.3 3.0 %own.1 = (f32[2,24,16,384]{3,2,1,0:T(8,128)S(1)}, f32[2,24,16,384]{3,2,1,0:T(8,128)S(1)}, f32[2,24,16,384]{3,2,1,0:T(8,128)S(1)}, f32[2,24,16,384]{3,2,1,0:T(8,1...) custom-call(f32[16,128]{1,0:T(8,128)S(1)} %table.1, ...), custom_call_target="tpu_custom_call" | custom-call | flops 10000000 | tf_op jit(solution)/shard_map/own/pallas_call | solution.py:680
  18.3 0.0 collective-permute-done.2.sfirst
  18.3 0.0 collective-permute-done.3.ssecond
  18.3 0.0 copy-start
  18.3 1.8 %near.1 = (f32[9,8,384]{2,1,0:T(8,128)S(1)}, f32[9,8,384]{2,1,0:T(8,128)S(1)}, f32[2,24,16,384]{3,2,1,0:T(8,128)S(1)}, f32[2,24,16,384]{3,2,1,0:T(8,128)S(1)}, f...) custom-call(f32[16,128]{1,0:T(8,128)S(1)} %table.1, ...), custom_call_target="tpu_custom_call", output_to_operand_aliasing={{2}: (3, {}), {3}: (4, {}), {4}: (5, {}), {5}: (6, {}), {6}... | custom-call | tf_op jit(solution)/shard_map/near/pallas_call | solution.py:680
  20.1 0.7 collective-permute-start.6
  20.8 3.7 %collective-permute-start.7 = (f32[9,8,384]{2,1,0:T(8,128)S(1)}, f32[9,8,384]{2,1,0:T(8,128)S(1)}, u32[]{:S(2)}, u32[]{:S(2)}) collective-permute-start(f32[9,8,384]{2,1,0:T(8,128)S(1)} %get-tuple-element.87), channel_id=1, source_target_pairs={{0,16},{32,48},{64,80},{96,112},{128,144},{160,176},{192,208},{224... | collective-permute-start | bytes 331784 | tf_op jit(solution)/shard_map/ppermute | solution.py:697
  24.5 0.0 copy-done
  24.5 0.6 inner.1
  25.1 0.0 collective-permute-done.6.first
  25.1 1.6 %collective-permute-done.7.second = f32[9,8,384]{2,1,0:T(8,128)S(1)} collective-permute-done((f32[9,8,384]{2,1,0:T(8,128)S(1)}, f32[9,8,384]{2,1,0:T(8,128)S(1)}, u32[]{:S(2)}, u32[]{:S(2)}) %collective-permute-start.7) | collective-permute-done | bytes 110624 | tf_op jit(solution)/shard_map/ppermute | solution.py:697
  26.7 0.9 %outer.1 = (f32[2,3,8,128]{3,2,1,0:T(8,128)S(1)}, f32[2,20,8,384]{3,2,1,0:T(8,128)S(1)}, f32[2,20,8,384]{3,2,1,0:T(8,128)S(1)}, f32[2,20,8,384]{3,2,1,0:T(8,128)...) custom-call(f32[9,8,384]{2,1,0:T(8,128)S(1)} %collective-permute-don, ...), custom_call_target="tpu_custom_call", output_to_operand_aliasing={{1}: (4, {}), {2}: (5, {}), {3}: (6, {}), {4}: (7, {}), {5}... | custom-call | tf_op jit(solution)/shard_map/outer/pallas_call | solution.py:680
  27.6 16.1 %all_to_all.10.gathered = f32[16,2,3,8,128]{4,3,2,1,0:T(8,128)S(1)} all-to-all(f32[16,2,3,8,128]{4,3,2,1,0:T(8,128)S(1)} %broadcast_in_dim.4), channel_id=1, replica_groups=mesh['gx'=16,'gy'=16] {'gx'}, dimensions={0} | all-to-all | bytes 786432 | tf_op jit(solution)/shard_map/all_to_all | solution.py:703
  43.7 1.5 %middle.1 = (f32[8,128]{1,0:T(8,128)S(1)}, f32[6,72,8,128]{3,2,1,0:T(8,128)S(1)}, f32[6,40,8,128]{3,2,1,0:T(8,128)S(1)}) custom-call(f32[16,2,3,8,128]{4,3,2,1,0:T(8,128)S(1)} %all_to_all.10.gathered), custom_call_target="tpu_custom_call" | custom-call | tf_op jit(solution)/shard_map/middle/pallas_call | solution.py:680
  45.3 19.6 %all_to_all.11.tiles = f32[16,8,128]{2,1,0:T(8,128)S(1)} all-to-all(f32[16,8,128]{2,1,0:T(8,128)S(1)} %broadcast_in_dim.5), channel_id=1, replica_groups=mesh['gx'=16,'gy'=16] {'gy'}, dimensions={0} | all-to-all | bytes 131072 | tf_op jit(solution)/shard_map/all_to_all | solution.py:703
  64.9 5.0 %up.1 = f32[2,8,2,16,256]{4,3,2,1,0:T(8,128)} custom-call(f32[16,8,128]{2,1,0:T(8,128)S(1)} %all_to_all.11.tiles, f32[6,72,8,128]{3,2,1,0:T(8,128)S(1)} %get-tuple-element.106.keep2, f32[6,40,8,128]{3,2,1,0:T(8,128)S(1)} %get-tuple-element.107.keep3, f32[16,2,16,256]{3,2,1,0:T(8,128)S(1)} %get-tuple-element.108.react, ...), custom_call_target="tpu_custom_call" | custom-call | tf_op jit(solution)/shard_map/up/pallas_call | solution.py:680
  (4 shorter events, 0.1 us)
Async XLA Ops:
  0.0 1.0 %copy-start.1 = (f32[2,16,16,256]{3,2,1,0:T(8,128)S(1)}, f32[2,16,16,256]{3,2,1,0:T(8,128)}, u32[]{:S(2)}) copy-start(f32[2,16,16,256]{3,2,1,0:T(8,128)} %param.7) | copy-start | bytes 1572868
  0.0 1.1 %copy-start.2 = (s32[16,16,256]{2,1,0:T(8,128)S(1)}, s32[16,16,256]{2,1,0:T(8,128)}, u32[]{:S(2)}) copy-start(s32[16,16,256]{2,1,0:T(8,128)} %param.5) | copy-start | bytes 786436
  0.0 15.2 %copy-start.3 = (f32[2,8]{1,0:T(2,128)S(1)}, f32[2,8]{1,0:T(2,128)}, u32[]{:S(2)}) copy-start(f32[2,8]{1,0:T(2,128)} %diff_ref.1) | copy-start | bytes 196
  1.4 9.5 %collective-permute-start = (f32[8,3,16,128]{3,2,1,0:T(8,128)S(1)}, f32[8,3,16,128]{3,2,1,0:T(8,128)S(1)}, u32[]{:S(2)}, u32[]{:S(2)}) collective-permute-start(f32[8,3,16,128]{3,2,1,0:T(8,128)S(1)} %get-tuple-element.63), channel_id=1, source_target_pairs={{1,2},{3,4},{5,6},{7,8},{9,10},{11,12},{13,14},{2,1},{4,3},{6,5},{... | collective-permute-start | bytes 589832 | tf_op jit(solution)/shard_map/ppermute | solution.py:697
  6.3 4.6 %collective-permute-start.1 = (f32[8,3,16,128]{3,2,1,0:T(8,128)S(1)}, f32[8,3,16,128]{3,2,1,0:T(8,128)S(1)}, u32[]{:S(2)}, u32[]{:S(2)}) collective-permute-start(f32[8,3,16,128]{3,2,1,0:T(8,128)S(1)} %get-tuple-element.64), channel_id=1, source_target_pairs={{0,1},{2,3},{4,5},{6,7},{8,9},{10,11},{12,13},{14,15},{1,0},{3,2},... | collective-permute-start | bytes 589832 | tf_op jit(solution)/shard_map/ppermute | solution.py:697
  6.5 8.8 %collective-permute-start.4 = (f32[10,16,256]{2,1,0:T(8,128)S(1)}, f32[10,16,256]{2,1,0:T(8,128)S(1)}, u32[]{:S(2)}, u32[]{:S(2)}) collective-permute-start(f32[10,16,256]{2,1,0:T(8,128)S(1)} %get-tuple-element.69), channel_id=1, source_target_pairs={{16,32},{48,64},{80,96},{112,128},{144,160},{176,192},{208,224},{3... | collective-permute-start | bytes 491528 | tf_op jit(solution)/shard_map/ppermute | solution.py:697
  7.2 8.1 %collective-permute-start.5 = (f32[10,16,256]{2,1,0:T(8,128)S(1)}, f32[10,16,256]{2,1,0:T(8,128)S(1)}, u32[]{:S(2)}, u32[]{:S(2)}) collective-permute-start(f32[10,16,256]{2,1,0:T(8,128)S(1)} %get-tuple-element.70), channel_id=1, source_target_pairs={{0,16},{32,48},{64,80},{96,112},{128,144},{160,176},{192,208},{224... | collective-permute-start | bytes 491528 | tf_op jit(solution)/shard_map/ppermute | solution.py:697
  11.0 7.2 %collective-permute-start.2 = (f32[10,16,128]{2,1,0:T(8,128)S(1)}, f32[10,16,128]{2,1,0:T(8,128)S(1)}, u32[]{:S(2)}, u32[]{:S(2)}) collective-permute-start(f32[10,16,128]{2,1,0:T(8,128)S(1)} %get-tuple-element.65), channel_id=1, source_target_pairs={{16,32},{48,64},{80,96},{112,128},{144,160},{176,192},{208,224},{3... | collective-permute-start | bytes 245768 | tf_op jit(solution)/shard_map/ppermute | solution.py:697
  11.7 6.6 %collective-permute-start.3 = (f32[10,16,128]{2,1,0:T(8,128)S(1)}, f32[10,16,128]{2,1,0:T(8,128)S(1)}, u32[]{:S(2)}, u32[]{:S(2)}) collective-permute-start(f32[10,16,128]{2,1,0:T(8,128)S(1)} %get-tuple-element.66), channel_id=1, source_target_pairs={{0,16},{32,48},{64,80},{96,112},{128,144},{160,176},{192,208},{224... | collective-permute-start | bytes 245768 | tf_op jit(solution)/shard_map/ppermute | solution.py:697
  18.3 6.2 %copy-start = (s32[2,16,16,256]{3,2,1,0:T(8,128)S(1)}, s32[2,16,16,256]{3,2,1,0:T(8,128)}, u32[]{:S(2)}) copy-start(s32[2,16,16,256]{3,2,1,0:T(8,128)} %param.4) | copy-start | bytes 1572868
  20.1 5.0 %collective-permute-start.6 = (f32[9,8,384]{2,1,0:T(8,128)S(1)}, f32[9,8,384]{2,1,0:T(8,128)S(1)}, u32[]{:S(2)}, u32[]{:S(2)}) collective-permute-start(f32[9,8,384]{2,1,0:T(8,128)S(1)} %get-tuple-element.86), channel_id=1, source_target_pairs={{16,32},{48,64},{80,96},{112,128},{144,160},{176,192},{208,224},{3... | collective-permute-start | bytes 331784 | tf_op jit(solution)/shard_map/ppermute | solution.py:697
  20.8 5.9 %collective-permute-start.7 = (f32[9,8,384]{2,1,0:T(8,128)S(1)}, f32[9,8,384]{2,1,0:T(8,128)S(1)}, u32[]{:S(2)}, u32[]{:S(2)}) collective-permute-start(f32[9,8,384]{2,1,0:T(8,128)S(1)} %get-tuple-element.87), channel_id=1, source_target_pairs={{0,16},{32,48},{64,80},{96,112},{128,144},{160,176},{192,208},{224... | collective-permute-start | bytes 331784 | tf_op jit(solution)/shard_map/ppermute | solution.py:697

commit v6 on v5

--- a/solution.py
+++ b/solution.py
@@ -658,7 +658,7 @@
     lax.fori_loop(0, 3, corrected_sweep, 0)
 
     def last(start):
-        for pair in zip(*(planes(keep0, q0, s, start, 8, 1) for s in range(2))):
+        for pair in zip(*(planes(keep0, q0, s, start, 4, 1) for s in range(2))):
             p = pair[0][0]
             a0, a1 = (
                 (here + keep0[4][s, p] * r)[:, :256] for s, (_, here, r) in enumerate(pair)
@@ -669,7 +669,7 @@
                 out[s, :, 0, x, :] = value[:8]
                 out[s, :, 1, x, :] = value[8:]
 
-    blocks(4, 20, 8, last)
+    blocks(4, 20, 4, last)
 
 
 def call(

time: 70.2 us -> 69.9 us (level)
  no operation moved by 1% of the time
where the time goes in v6:
time: 69.9 us; the launch traced here: 69.7 us
  blocking collectives  35.7 us (51%)
  starting transfers between devices  18 us (26%)
  Pallas kernels  13.1 us (19%)
  waiting for transfers between devices  1.57 us (2%)
  local copies, waits for them, and re-layouts  1.14 us (2%)
    all_to_all x2, blocking collectives, everyone(): return lax.all_to_all(copies, axis, split_axis=0, concat_axis=0, tiled=True)  35.7 us
    ppermute x8, starting transfers between devices, swap(): return lax.ppermute(block, axis, pairs + [(j, i) for i, j in pairs])  18 us
    pallas_call x11, Pallas kernels, call(): pl.pallas_call(kernel, out_shape=[jax.ShapeDtypeStruct(o, d) for o, d in...  13.1 us
    ppermute x8, waiting for transfers between devices, swap(): return lax.ppermute(block, axis, pairs + [(j, i) for i, j in pairs])  1.57 us
  transfers between devices with their start and end apart: 8, of which 1 were waited for; matrix products, arithmetic and copies ran while one was open for 0% of the time, Pallas kernels for 5%

profile of v6, /device:TPU:1, one launch (start us, length us, event | category | flops | bytes accessed | tf_op | source)
XLA Modules:
  0.0 69.7 jit_solution(15010843091897989199)
XLA Ops:
  0.0 0.0 copy-start.1
  0.0 0.0 copy-start.2
  0.0 0.0 copy-start.3
  0.0 1.0 %copy-done.1 = f32[2,16,16,256]{3,2,1,0:T(8,128)S(1)} copy-done((f32[2,16,16,256]{3,2,1,0:T(8,128)S(1)}, f32[2,16,16,256]{3,2,1,0:T(8,128)}, u32[]{:S(2)}) %copy-start.1) | copy-done | bytes 524312
  1.0 0.1 copy-done.2
  1.1 0.3 turn.1
  1.4 4.9 %collective-permute-start = (f32[8,3,16,128]{3,2,1,0:T(8,128)S(1)}, f32[8,3,16,128]{3,2,1,0:T(8,128)S(1)}, u32[]{:S(2)}, u32[]{:S(2)}) collective-permute-start(f32[8,3,16,128]{3,2,1,0:T(8,128)S(1)} %get-tuple-element.63), channel_id=1, source_target_pairs={{1,2},{3,4},{5,6},{7,8},{9,10},{11,12},{13,14},{2,1},{4,3},{6,5},{... | collective-permute-start | bytes 589832 | tf_op jit(solution)/shard_map/ppermute | solution.py:697
  6.3 0.1 collective-permute-start.1
  6.5 0.7 collective-permute-start.4
  7.2 3.7 %collective-permute-start.5 = (f32[10,16,256]{2,1,0:T(8,128)S(1)}, f32[10,16,256]{2,1,0:T(8,128)S(1)}, u32[]{:S(2)}, u32[]{:S(2)}) collective-permute-start(f32[10,16,256]{2,1,0:T(8,128)S(1)} %get-tuple-element.70), channel_id=1, source_target_pairs={{0,16},{32,48},{64,80},{96,112},{128,144},{160,176},{192,208},{224... | collective-permute-start | bytes 491528 | tf_op jit(solution)/shard_map/ppermute | solution.py:697
  10.9 0.0 collective-permute-done.across
  10.9 0.0 collective-permute-done.1.inside
  10.9 0.1 edge.1
  11.0 0.7 collective-permute-start.2
  11.7 3.5 %collective-permute-start.3 = (f32[10,16,128]{2,1,0:T(8,128)S(1)}, f32[10,16,128]{2,1,0:T(8,128)S(1)}, u32[]{:S(2)}, u32[]{:S(2)}) collective-permute-start(f32[10,16,128]{2,1,0:T(8,128)S(1)} %get-tuple-element.66), channel_id=1, source_target_pairs={{0,16},{32,48},{64,80},{96,112},{128,144},{160,176},{192,208},{224... | collective-permute-start | bytes 245768 | tf_op jit(solution)/shard_map/ppermute | solution.py:697
  15.2 0.0 copy-done.3
  15.2 0.1 table.1
  15.3 0.0 collective-permute-done.4.mfirst
  15.3 0.0 collective-permute-done.5.msecond
  15.3 3.0 %own.1 = (f32[2,24,16,384]{3,2,1,0:T(8,128)S(1)}, f32[2,24,16,384]{3,2,1,0:T(8,128)S(1)}, f32[2,24,16,384]{3,2,1,0:T(8,128)S(1)}, f32[2,24,16,384]{3,2,1,0:T(8,1...) custom-call(f32[16,128]{1,0:T(8,128)S(1)} %table.1, ...), custom_call_target="tpu_custom_call" | custom-call | flops 10000000 | tf_op jit(solution)/shard_map/own/pallas_call | solution.py:680
  18.3 0.0 collective-permute-done.2.sfirst
  18.3 0.0 collective-permute-done.3.ssecond
  18.3 0.0 copy-start
  18.3 1.8 %near.1 = (f32[9,8,384]{2,1,0:T(8,128)S(1)}, f32[9,8,384]{2,1,0:T(8,128)S(1)}, f32[2,24,16,384]{3,2,1,0:T(8,128)S(1)}, f32[2,24,16,384]{3,2,1,0:T(8,128)S(1)}, f...) custom-call(f32[16,128]{1,0:T(8,128)S(1)} %table.1, ...), custom_call_target="tpu_custom_call", output_to_operand_aliasing={{2}: (3, {}), {3}: (4, {}), {4}: (5, {}), {5}: (6, {}), {6}... | custom-call | tf_op jit(solution)/shard_map/near/pallas_call | solution.py:680
  20.1 0.7 collective-permute-start.6
  20.8 3.7 %collective-permute-start.7 = (f32[9,8,384]{2,1,0:T(8,128)S(1)}, f32[9,8,384]{2,1,0:T(8,128)S(1)}, u32[]{:S(2)}, u32[]{:S(2)}) collective-permute-start(f32[9,8,384]{2,1,0:T(8,128)S(1)} %get-tuple-element.87), channel_id=1, source_target_pairs={{0,16},{32,48},{64,80},{96,112},{128,144},{160,176},{192,208},{224... | collective-permute-start | bytes 331784 | tf_op jit(solution)/shard_map/ppermute | solution.py:697
  24.5 0.0 copy-done
  24.5 0.6 inner.1
  25.1 0.0 collective-permute-done.6.first
  25.1 1.6 %collective-permute-done.7.second = f32[9,8,384]{2,1,0:T(8,128)S(1)} collective-permute-done((f32[9,8,384]{2,1,0:T(8,128)S(1)}, f32[9,8,384]{2,1,0:T(8,128)S(1)}, u32[]{:S(2)}, u32[]{:S(2)}) %collective-permute-start.7) | collective-permute-done | bytes 110624 | tf_op jit(solution)/shard_map/ppermute | solution.py:697
  26.7 0.9 %outer.1 = (f32[2,3,8,128]{3,2,1,0:T(8,128)S(1)}, f32[2,20,8,384]{3,2,1,0:T(8,128)S(1)}, f32[2,20,8,384]{3,2,1,0:T(8,128)S(1)}, f32[2,20,8,384]{3,2,1,0:T(8,128)...) custom-call(f32[9,8,384]{2,1,0:T(8,128)S(1)} %collective-permute-don, ...), custom_call_target="tpu_custom_call", output_to_operand_aliasing={{1}: (4, {}), {2}: (5, {}), {3}: (6, {}), {4}: (7, {}), {5}... | custom-call | tf_op jit(solution)/shard_map/outer/pallas_call | solution.py:680
  27.6 16.1 %all_to_all.10.gathered = f32[16,2,3,8,128]{4,3,2,1,0:T(8,128)S(1)} all-to-all(f32[16,2,3,8,128]{4,3,2,1,0:T(8,128)S(1)} %broadcast_in_dim.4), channel_id=1, replica_groups=mesh['gx'=16,'gy'=16] {'gx'}, dimensions={0} | all-to-all | bytes 786432 | tf_op jit(solution)/shard_map/all_to_all | solution.py:703
  43.7 1.5 %middle.1 = (f32[8,128]{1,0:T(8,128)S(1)}, f32[6,72,8,128]{3,2,1,0:T(8,128)S(1)}, f32[6,40,8,128]{3,2,1,0:T(8,128)S(1)}) custom-call(f32[16,2,3,8,128]{4,3,2,1,0:T(8,128)S(1)} %all_to_all.10.gathered), custom_call_target="tpu_custom_call" | custom-call | tf_op jit(solution)/shard_map/middle/pallas_call | solution.py:680
  45.3 19.6 %all_to_all.11.tiles = f32[16,8,128]{2,1,0:T(8,128)S(1)} all-to-all(f32[16,8,128]{2,1,0:T(8,128)S(1)} %broadcast_in_dim.5), channel_id=1, replica_groups=mesh['gx'=16,'gy'=16] {'gy'}, dimensions={0} | all-to-all | bytes 131072 | tf_op jit(solution)/shard_map/all_to_all | solution.py:703
  64.9 4.8 %up.1 = f32[2,8,2,16,256]{4,3,2,1,0:T(8,128)} custom-call(f32[16,8,128]{2,1,0:T(8,128)S(1)} %all_to_all.11.tiles, f32[6,72,8,128]{3,2,1,0:T(8,128)S(1)} %get-tuple-element.106.keep2, f32[6,40,8,128]{3,2,1,0:T(8,128)S(1)} %get-tuple-element.107.keep3, f32[16,2,16,256]{3,2,1,0:T(8,128)S(1)} %get-tuple-element.108.react, ...), custom_call_target="tpu_custom_call" | custom-call | tf_op jit(solution)/shard_map/up/pallas_call | solution.py:680
  (4 shorter events, 0.1 us)
Async XLA Ops:
  0.0 1.0 %copy-start.1 = (f32[2,16,16,256]{3,2,1,0:T(8,128)S(1)}, f32[2,16,16,256]{3,2,1,0:T(8,128)}, u32[]{:S(2)}) copy-start(f32[2,16,16,256]{3,2,1,0:T(8,128)} %param.7) | copy-start | bytes 1572868
  0.0 1.1 %copy-start.2 = (s32[16,16,256]{2,1,0:T(8,128)S(1)}, s32[16,16,256]{2,1,0:T(8,128)}, u32[]{:S(2)}) copy-start(s32[16,16,256]{2,1,0:T(8,128)} %param.5) | copy-start | bytes 786436
  0.0 15.2 %copy-start.3 = (f32[2,8]{1,0:T(2,128)S(1)}, f32[2,8]{1,0:T(2,128)}, u32[]{:S(2)}) copy-start(f32[2,8]{1,0:T(2,128)} %diff_ref.1) | copy-start | bytes 196
  1.4 9.5 %collective-permute-start = (f32[8,3,16,128]{3,2,1,0:T(8,128)S(1)}, f32[8,3,16,128]{3,2,1,0:T(8,128)S(1)}, u32[]{:S(2)}, u32[]{:S(2)}) collective-permute-start(f32[8,3,16,128]{3,2,1,0:T(8,128)S(1)} %get-tuple-element.63), channel_id=1, source_target_pairs={{1,2},{3,4},{5,6},{7,8},{9,10},{11,12},{13,14},{2,1},{4,3},{6,5},{... | collective-permute-start | bytes 589832 | tf_op jit(solution)/shard_map/ppermute | solution.py:697
  6.3 4.6 %collective-permute-start.1 = (f32[8,3,16,128]{3,2,1,0:T(8,128)S(1)}, f32[8,3,16,128]{3,2,1,0:T(8,128)S(1)}, u32[]{:S(2)}, u32[]{:S(2)}) collective-permute-start(f32[8,3,16,128]{3,2,1,0:T(8,128)S(1)} %get-tuple-element.64), channel_id=1, source_target_pairs={{0,1},{2,3},{4,5},{6,7},{8,9},{10,11},{12,13},{14,15},{1,0},{3,2},... | collective-permute-start | bytes 589832 | tf_op jit(solution)/shard_map/ppermute | solution.py:697
  6.5 8.8 %collective-permute-start.4 = (f32[10,16,256]{2,1,0:T(8,128)S(1)}, f32[10,16,256]{2,1,0:T(8,128)S(1)}, u32[]{:S(2)}, u32[]{:S(2)}) collective-permute-start(f32[10,16,256]{2,1,0:T(8,128)S(1)} %get-tuple-element.69), channel_id=1, source_target_pairs={{16,32},{48,64},{80,96},{112,128},{144,160},{176,192},{208,224},{3... | collective-permute-start | bytes 491528 | tf_op jit(solution)/shard_map/ppermute | solution.py:697
  7.2 8.1 %collective-permute-start.5 = (f32[10,16,256]{2,1,0:T(8,128)S(1)}, f32[10,16,256]{2,1,0:T(8,128)S(1)}, u32[]{:S(2)}, u32[]{:S(2)}) collective-permute-start(f32[10,16,256]{2,1,0:T(8,128)S(1)} %get-tuple-element.70), channel_id=1, source_target_pairs={{0,16},{32,48},{64,80},{96,112},{128,144},{160,176},{192,208},{224... | collective-permute-start | bytes 491528 | tf_op jit(solution)/shard_map/ppermute | solution.py:697
  11.0 7.2 %collective-permute-start.2 = (f32[10,16,128]{2,1,0:T(8,128)S(1)}, f32[10,16,128]{2,1,0:T(8,128)S(1)}, u32[]{:S(2)}, u32[]{:S(2)}) collective-permute-start(f32[10,16,128]{2,1,0:T(8,128)S(1)} %get-tuple-element.65), channel_id=1, source_target_pairs={{16,32},{48,64},{80,96},{112,128},{144,160},{176,192},{208,224},{3... | collective-permute-start | bytes 245768 | tf_op jit(solution)/shard_map/ppermute | solution.py:697
  11.7 6.6 %collective-permute-start.3 = (f32[10,16,128]{2,1,0:T(8,128)S(1)}, f32[10,16,128]{2,1,0:T(8,128)S(1)}, u32[]{:S(2)}, u32[]{:S(2)}) collective-permute-start(f32[10,16,128]{2,1,0:T(8,128)S(1)} %get-tuple-element.66), channel_id=1, source_target_pairs={{0,16},{32,48},{64,80},{96,112},{128,144},{160,176},{192,208},{224... | collective-permute-start | bytes 245768 | tf_op jit(solution)/shard_map/ppermute | solution.py:697
  18.3 6.2 %copy-start = (s32[2,16,16,256]{3,2,1,0:T(8,128)S(1)}, s32[2,16,16,256]{3,2,1,0:T(8,128)}, u32[]{:S(2)}) copy-start(s32[2,16,16,256]{3,2,1,0:T(8,128)} %param.4) | copy-start | bytes 1572868
  20.1 5.0 %collective-permute-start.6 = (f32[9,8,384]{2,1,0:T(8,128)S(1)}, f32[9,8,384]{2,1,0:T(8,128)S(1)}, u32[]{:S(2)}, u32[]{:S(2)}) collective-permute-start(f32[9,8,384]{2,1,0:T(8,128)S(1)} %get-tuple-element.86), channel_id=1, source_target_pairs={{16,32},{48,64},{80,96},{112,128},{144,160},{176,192},{208,224},{3... | collective-permute-start | bytes 331784 | tf_op jit(solution)/shard_map/ppermute | solution.py:697
  20.8 5.9 %collective-permute-start.7 = (f32[9,8,384]{2,1,0:T(8,128)S(1)}, f32[9,8,384]{2,1,0:T(8,128)S(1)}, u32[]{:S(2)}, u32[]{:S(2)}) collective-permute-start(f32[9,8,384]{2,1,0:T(8,128)S(1)} %get-tuple-element.87), channel_id=1, source_target_pairs={{0,16},{32,48},{64,80},{96,112},{128,144},{160,176},{192,208},{224... | collective-permute-start | bytes 331784 | tf_op jit(solution)/shard_map/ppermute | solution.py:697
